TPU v7x, 256 devices: a whole 4x4x8 slice. The times are simulated.
256 devices in a mesh: chain: 32 (over z, x_hi, core), tok: 8 (over x_lo, y).
Axes of the slice: x: 4 (x_hi: 2, x_lo: 2; x = x_hi * 2 + x_lo), y: 4, z: 8, core: 2. Of those that a mesh axis runs over, the one named last changes fastest.
Arguments:
- queries: bfloat16 [524288, 128], P(('chain', 'tok')), may hold values from -6 to 6
- keys: bfloat16 [524288, 128], P(('chain', 'tok')), may hold values from -6 to 6
- values: bfloat16 [524288, 128], P(('chain', 'tok')), may hold values from -6 to 6
Outputs:
- attended: bfloat16 [524288, 128], P(('chain', 'tok'))
All inputs are finite; a program needn't handle non-finite values.
Results may differ from a plain program's by a relative error of at most 0.0058.
Values may be sent and summed in bfloat16 or wider, within the bound.
No kernel may reach another device: no remote copies, remote signals or barrier semaphores. Data moves between devices by JAX's collectives and lax.ppermute only.
A program may use at most 64 MiB of HBM per device.

v0:
```python
import math

import jax
import jax.numpy as jnp
import numpy as np
from jax import lax
from jax.sharding import Mesh
from jax.sharding import PartitionSpec as P

HD = 64
HEADS = 2
F = 2080
CHAIN = ("chain_0", "chain_1", "chain_2")
CHAIN_TOK = ("chain_0", "chain_1", "chain_2", "tok")


def in_blocks(value, dim, length):
    dims = value.shape
    parts = value.reshape(*dims[:dim], length, dims[dim] // length, *dims[dim + 1 :])
    return jnp.moveaxis(parts, dim, 0)


def summed_on_arrival(value, axis, dim):
    length = lax.axis_size(axis)
    parts = lax.all_to_all(in_blocks(value, dim, length), axis, 0, 0, tiled=True)
    return jnp.sum(parts, axis=0)


def neutral_like(value, identity):
    return jnp.broadcast_to(jnp.asarray(identity, value.dtype), value.shape)


def entering(value, axes, combine, identity):
    before = start = neutral_like(value, identity)
    running = value
    for axis in reversed(axes):
        length, here = (lax.axis_size(axis), lax.axis_index(axis))
        pieces = lax.all_gather(running, axis)
        inside, running = (start, start)
        for k in range(length):
            passed = k < here
            running = combine(running, pieces[k])
            inside = jnp.where(passed, running, inside)
        before = combine(inside, before)
    return before


def in_order(parts, dim):
    parts = jnp.moveaxis(parts, 0, dim)
    dims = parts.shape
    return parts.reshape(*dims[:dim], dims[dim] * dims[dim + 1], *dims[dim + 2 :])


def copy_for_each(value, axis):
    length = lax.axis_size(axis)
    return lax.all_to_all(
        jnp.broadcast_to(value[None], (length, *value.shape)), axis, 0, 0, tiled=True
    )


def gathered_copies(value, axis, dim):
    return in_order(copy_for_each(value, axis), dim)


def tables(width):
    first, second = np.triu_indices(width)
    places = np.arange(width)[:, None]
    first_pick = jnp.asarray((places == first[None, :]).astype(np.float32), jnp.bfloat16)
    second_pick = jnp.asarray((places == second[None, :]).astype(np.float32), jnp.bfloat16)
    scaling = jnp.asarray(np.where(first < second, math.sqrt(2.0), 1.0).astype(np.float32))
    return (first_pick, second_pick, scaling)


def expand(vectors, first_pick, second_pick, scaling):
    left = jnp.einsum("thd,df->hft", vectors, first_pick, preferred_element_type=jnp.bfloat16)
    right = jnp.einsum("thd,df->hft", vectors, second_pick, preferred_element_type=jnp.bfloat16)
    product = left.astype(jnp.float32) * right.astype(jnp.float32) * scaling[None, :, None]
    return product.astype(jnp.bfloat16)


def read_state(query_heads, piece, tables_all):
    first_pick, second_pick, scaling = tables_all
    count = piece.shape[1]
    first_part = lax.slice_in_dim(first_pick, 0, count, axis=1)
    second_part = lax.slice_in_dim(second_pick, 0, count, axis=1)
    scale_part = lax.slice_in_dim(scaling, 0, count, axis=0)
    feats = expand(query_heads, first_part, second_part, scale_part)
    state = piece[0].reshape(count, 2, HD)
    part = jnp.einsum("hft,fhd->thd", feats, state, preferred_element_type=jnp.float32)
    pieces = part.reshape(query_heads.shape[0], 2 * HD)
    return pieces


def add_states(earlier, later):
    return earlier + later


def on_device(queries, keys, values):
    tables_all = tables(HD)
    first_pick, second_pick, scaling = tables_all
    length = queries.shape[0]
    query_heads = queries.reshape(length, HEADS, HD)
    key_heads = keys.reshape(length, HEADS, HD)
    value_heads = values.reshape(length, HEADS, HD)
    feats = expand(key_heads, first_pick, second_pick, scaling)
    state = jnp.einsum("hft,thd->fhd", feats, value_heads, preferred_element_type=jnp.float32)
    states = [state.reshape(F, 2 * HD)]
    local = jnp.stack(states)
    share = summed_on_arrival(local, "tok", 1)
    before = entering(share, CHAIN, add_states, jnp.zeros_like(share))
    inclusive = (before + share).astype(jnp.bfloat16)
    gathered = read_state(query_heads, gathered_copies(inclusive, "tok", 1), tables_all)
    count = (lax.axis_index(CHAIN) + 1).astype(jnp.float32) * (length * lax.axis_size("tok"))
    return (gathered / (HD * jnp.sqrt(count))).astype(jnp.bfloat16)


def solution(mesh):
    torus = Mesh(
        mesh.devices.reshape(8, 2, 2, mesh.shape["tok"]), ("chain_0", "chain_1", "chain_2", "tok")
    )
    in_specs = (P(CHAIN_TOK, None), P(CHAIN_TOK, None), P(CHAIN_TOK, None))
    out_specs = P(CHAIN_TOK, None)
    return jax.shard_map(
        on_device, mesh=torus, in_specs=in_specs, out_specs=out_specs, check_vma=False
    )
```

profile of v0, /device:TPU:2, one launch (start us, length us, event | category | flops | bytes accessed | tf_op | source)
XLA Modules:
  0.0 144.8 jit_solution(12849169256115107587)
XLA Ops:
  6.5 0.0 copy-start.4
  6.5 0.0 copy-start.2
  6.5 0.0 all-gather.6.cloned.1.call-start
  6.5 1.3 copy.13
  7.8 1.2 copy.14
  9.1 9.3 %fusion.28 = bf16[2080,2048,2]{1,0,2:T(8,128)(2,1)} fusion(bf16[64,2080,1]{1,0,2:T(8,128)(2,1)} %constant.47, bf16[2048,2,64]{0,2,1:T(8,128)(2,1)S(1)} %bitcast.63), kind=kOutput, calls=%fused_computation.31 | convolution fusion | flops 1090519040 | bytes 17829888 | tf_op jit(solution)/shard_map/thd,df->hft/dot_general | solution.py:75
  18.3 0.0 copy-done.4
  18.4 0.0 copy-done.2
  18.4 0.0 copy-start.1
  18.4 0.0 copy-start
  18.4 14.2 %fusion.12 = f32[2080,2,64]{0,2,1:T(8,128)} fusion(bf16[2048,2,64]{0,2,1:T(8,128)(2,1)S(1)} %bitcast.67, bf16[2080,2048,2]{1,0,2:T(8,128)(2,1)} %fusion.28, f32[2080]{0:T(1024)S(1)} %copy-done.4, bf16[64,2080,1]{1,0,2:T(8,128)(2,1)S(1)} %copy-done.2, bf16[2048,2,64]{0,2,1:T(8,128)(2,1)S(1)} %bitcast.64), kind=kOutput, calls=%fused_computation.10 | convolution fusion | flops 2223636480 | bytes 19427456 | tf_op jit(solution)/shard_map/hft,thd->fhd/dot_general | solution.py:106
  32.6 2.1 %transpose_reshape_stack_reshape.3 = f32[8,1,260,128]{2,0,3,1:T(8,128)S(1)} reshape(f32[2080,2,64]{0,2,1:T(8,128)} %fusion.12) | data formatting | bytes 2129920 | tf_op jit(solution)/shard_map/transpose;reshape;stack;reshape | solution.py:20
  34.7 0.9 copy.15
  35.5 20.5 %all_to_all.10 = f32[8,1,260,128]{3,1,2,0:T(1,128)S(1)} all-to-all(f32[8,1,260,128]{3,1,2,0:T(1,128)S(1)} %copy.15), channel_id=1, replica_groups=mesh['chain_0'=8,'chain_1'=2,'chain_2'=2,'tok'=8] {'tok'}, dimensions={0} | all-to-all | bytes 2129920 | tf_op jit(solution)/shard_map/all_to_all | solution.py:25
  56.1 0.8 reduce_sum.9
  56.8 2.0 %all-gather.2 = f32[2,260,128]{2,1,0:T(8,128)S(1)} all-gather(f32[1,260,128]{2,1,0:T(8,128)S(1)} %bitcast.65), channel_id=2, replica_groups=mesh['chain_0'=8,'chain_1'=2,'chain_2'=2,'tok'=8] {'chain_2'}, dimensions={0}, use_global_device_ids=true | all-gather | bytes 399360 | tf_op jit(solution)/shard_map/all_gather | solution.py:38
  58.9 7.8 %all-gather.3 = f32[2,260,128]{2,1,0:T(8,128)S(1)} all-gather(f32[1,260,128]{2,1,0:T(8,128)S(1)} %slice_add_fusion.1), channel_id=3, replica_groups=mesh['chain_0'=8,'chain_1'=2,'chain_2'=2,'tok'=8] {'chain_1'}, dimensions={0}, use_global_device_ids=true | all-gather | bytes 399360 | tf_op jit(solution)/shard_map/all_gather | solution.py:38
  66.7 0.8 copy.16
  67.5 0.0 all-gather.6.cloned.1.call-update
  67.6 0.0 copy-done.1
  67.6 0.2 copy.26
  67.8 0.0 copy-start.3
  67.8 40.2 %all-gather.6.cloned.1.call-done = f32[8,1,260,128]{3,1,2,0:T(1,128)} async-done(((f32[1,1,260,128]{3,1,2,0:T(1,128)}), f32[8,1,260,128]{3,1,2,0:T(1,128)}) %all-gather.6.cloned.1.call-update) | async-done | bytes 1064976 | tf_op jit(solution)/shard_map/all_gather | solution.py:38
  108.0 1.4 fusion.27
  109.4 0.2 fusion.26
  109.5 0.9 broadcast_in_dim.15
  110.4 5.7 %all-to-all-start.1 = ((bf16[8,1,260,128]{3,2,1,0:T(8,128)(2,1)}), bf16[8,1,260,128]{3,2,1,0:T(8,128)(2,1)S(1)}, u32[]{:S(2)}, u32[]{:S(2)}) async-start(bf16[8,1,260,128]{3,2,1,0:T(8,128)(2,1)} %broadcast_in_dim.15), calls=%async_computation.1 | async-start | bytes 1081344 | tf_op jit(solution)/shard_map/all_to_all | solution.py:56
  116.1 0.0 copy-done
  116.2 8.3 %fusion.29 = bf16[2080,2048,2]{1,0,2:T(8,128)(2,1)} fusion(bf16[64,2080,1]{1,0,2:T(8,128)(2,1)S(1)} %copy-done, bf16[2048,2,64]{0,2,1:T(8,128)(2,1)S(1)} %bitcast.61), kind=kOutput, calls=%fused_computation.32 | convolution fusion | flops 1090519040 | bytes 17829888 | tf_op jit(solution)/shard_map/thd,df->hft/dot_general | solution.py:75
  124.4 0.0 all-to-all-done.1
  124.4 0.5 copy.25
  125.0 0.6 reshape_squeeze_reshape_transpose.3
  125.6 0.0 copy-done.3
  125.6 11.4 %fusion.18 = bf16[2,64,2048]{2,1,0:T(8,128)(2,1)S(1)} fusion(bf16[2080,2,64]{0,2,1:T(8,128)(2,1)S(1)} %reshape_squeeze_reshape_transpose.3, bf16[2080,2048,2]{1,0,2:T(8,128)(2,1)} %fusion.29, f32[2080]{0:T(1024)S(1)} %copy-done.4, bf16[64,2080,1]{1,0,2:T(8,128)(2,1)S(1)} %copy-done.3, bf16[2048,2,64]{0,2,1:T(8,128)(2,1)S(1)} %bitcast.62, f32[]{:T(128)S(6)} %mul_shard_map.3), kind=kOutput, calls=%fused_computation.12 | convolution fusion | flops 2224160768 | bytes 18894980 | tf_op jit(solution)/shard_map/hft,fhd->thd/dot_general | solution.py:89
  136.9 1.0 copy.27
  (2 shorter events, 0.0 us)
Async XLA Ops:
  6.5 11.8 %copy-start.4 = (f32[2080]{0:T(1024)S(1)}, f32[2080]{0:T(1024)}, u32[]{:S(2)}) copy-start(f32[2080]{0:T(1024)} %constant.46.clone) | copy-start | bytes 24964
  6.5 11.8 %copy-start.2 = (bf16[64,2080,1]{1,0,2:T(8,128)(2,1)S(1)}, bf16[64,2080,1]{1,0,2:T(8,128)(2,1)}, u32[]{:S(2)}) copy-start(bf16[64,2080,1]{1,0,2:T(8,128)(2,1)} %constant.48) | copy-start | bytes 798724
  6.5 101.5 %all-gather.6.cloned.1.call-start = ((), (), s32[]{:S(2)}) async-start(), calls=%async_computation.2 | async-start | bytes 1198080 | tf_op jit(solution)/shard_map/all_gather | solution.py:38
  18.4 49.2 %copy-start.1 = (bf16[2048,128]{1,0:T(8,128)(2,1)S(1)}, bf16[2048,128]{1,0:T(8,128)(2,1)}, u32[]{:S(2)}) copy-start(bf16[2048,128]{1,0:T(8,128)(2,1)} %param.6) | copy-start | bytes 1572868
  18.4 97.8 %copy-start = (bf16[64,2080,1]{1,0,2:T(8,128)(2,1)S(1)}, bf16[64,2080,1]{1,0,2:T(8,128)(2,1)}, u32[]{:S(2)}) copy-start(bf16[64,2080,1]{1,0,2:T(8,128)(2,1)} %constant.47) | copy-start | bytes 798724
  67.8 57.7 %copy-start.3 = (bf16[64,2080,1]{1,0,2:T(8,128)(2,1)S(1)}, bf16[64,2080,1]{1,0,2:T(8,128)(2,1)}, u32[]{:S(2)}) copy-start(bf16[64,2080,1]{1,0,2:T(8,128)(2,1)} %constant.48) | copy-start | bytes 798724
  110.4 14.0 %all-to-all-start.1 = ((bf16[8,1,260,128]{3,2,1,0:T(8,128)(2,1)}), bf16[8,1,260,128]{3,2,1,0:T(8,128)(2,1)S(1)}, u32[]{:S(2)}, u32[]{:S(2)}) async-start(bf16[8,1,260,128]{3,2,1,0:T(8,128)(2,1)} %broadcast_in_dim.15), calls=%async_computation.1 | async-start | bytes 1081344 | tf_op jit(solution)/shard_map/all_to_all | solution.py:56
Sparse Core Ops, SparseCore 0:
  67.6 40.3 all-gather.5
where the time goes:
time: 145 us
  matrix products  43.1 us (30%)
  waiting for transfers between devices  40.2 us (28%)
  blocking collectives  30.3 us (21%)
  between operations  13.6 us (9%)
  local copies, waits for them, and re-layouts  10.9 us (8%)
  starting transfers between devices  5.75 us (4%)
    all_gather x1, waiting for transfers between devices, entering(): pieces = lax.all_gather(running, axis)  40.2 us
    all_to_all x1, blocking collectives, summed_on_arrival(): lax.all_to_all(in_blocks(value, dim, length), axis, 0, 0, tiled=True)  20.5 us
    dot_general x2, matrix products, expand(): jnp.einsum('thd,df->hft', vectors, first_pick, preferred_element_type=jnp...  17.5 us
    dot_general x1, matrix products, on_device(): jnp.einsum('hft,thd->fhd', feats, value_heads, preferred_element_type=jnp...  14.2 us
    dot_general x1, matrix products, read_state(): jnp.einsum('hft,fhd->thd', feats, state, preferred_element_type=jnp.float32)  11.4 us
    all_gather x2, blocking collectives, entering(): pieces = lax.all_gather(running, axis)  9.82 us
    all_to_all x1, starting transfers between devices, copy_for_each(): lax.all_to_all(jnp.broadcast_to(value[None], (length, *value.shape)), axi...  5.75 us
    another operation x2, local copies, waits for them, and re-layouts, in_blocks(): return jnp.moveaxis(parts, dim, 0)  2.94 us
  transfers between devices with their start and end apart: 2, of which 1 were waited for; matrix products, arithmetic and copies ran while one was open for 6% of the time, Pallas kernels for 0%

commit v1 on v0

v1 whole, which is shorter than its diff:
```python
import functools

import jax
import jax.numpy as jnp
from jax import lax
from jax.experimental import pallas as pl
from jax.experimental.pallas import tpu as pltpu
from jax.sharding import Mesh
from jax.sharding import PartitionSpec as P

HD = 64
HEADS = 2
WIDE = HEADS * HD
BLOCK = 16
BLOCKS = HD // BLOCK
HALF = BLOCK // 2
PAIRS = [(a, b) for a in range(BLOCKS) for b in range(a + 1, BLOCKS)]
SAME = [(a, a) for a in range(BLOCKS)]
ROWS = (HALF + 1) * BLOCK * len(SAME) + BLOCK * BLOCK * len(PAIRS)

PLANE = ("pair", "core", "near", "row")
EVERY = ("depth",) + PLANE


def pieces():
    first = 0
    for turn in range(BLOCK):
        same = SAME if turn <= HALF else []
        yield turn, same, PAIRS, first
        first += BLOCK * (len(same) + len(PAIRS))


def turned(flat, plain, head, turn, lanes):
    out = []
    for block in range(BLOCKS):
        rows = pl.ds(head * HD + block * BLOCK, BLOCK)
        if turn == 0:
            out.append(plain[rows, lanes])
        else:
            out.append(pltpu.roll(flat[rows, lanes], BLOCK - turn, 0).astype(jnp.bfloat16))
    return out


def features(flat, plain, head, turn, pairs, lanes):
    second = turned(flat, plain, head, turn, lanes)
    first = [plain[pl.ds(head * HD + b * BLOCK, BLOCK), lanes] for b in range(BLOCKS)]
    return [first[a] * second[b] for a, b in pairs]


def state_kernel(keys, values, out, flat, plain):
    wide = keys[...].astype(jnp.float32).T
    flat[...] = wide
    plain[...] = wide.astype(jnp.bfloat16)
    lanes = pl.ds(0, keys.shape[0])
    left = lax.broadcasted_iota(jnp.int32, (1, WIDE), 1) < HD
    for turn, same, pairs, row in pieces():
        count = BLOCK * (len(same) + len(pairs))
        sums = []
        for head in range(HEADS):
            feats = jnp.concatenate(features(flat, plain, head, turn, same + pairs, lanes), 0)
            sums.append(jnp.dot(feats, values[...], preferred_element_type=jnp.float32))
        total = jnp.where(left, sums[0], sums[1])
        once = BLOCK * len(same) if turn in (0, HALF) else 0
        if once:
            out[pl.ds(row, once), :] = total[:once].astype(out.dtype)
        out[pl.ds(row + once, count - once), :] = (2.0 * total[once:]).astype(out.dtype)
    if out.shape[0] > ROWS:
        out[pl.ds(ROWS, out.shape[0] - ROWS), :] = jnp.zeros((out.shape[0] - ROWS, WIDE), out.dtype)


def read_kernel(tile, scale, queries, state, out, flat, plain, feats):
    turned_state = state[...].astype(jnp.float32).T.astype(jnp.bfloat16)
    wide = queries[...].astype(jnp.float32).T
    flat[...] = wide
    plain[...] = wide.astype(jnp.bfloat16)
    factor = scale[0]
    for step in range(queries.shape[0] // tile):
        lanes = pl.ds(step * tile, tile)
        both = []
        for head in range(HEADS):
            for turn, same, pairs, row in pieces():
                for k, block in enumerate(features(flat, plain, head, turn, same + pairs, lanes)):
                    feats[pl.ds(row + BLOCK * k, BLOCK), lanes] = block
            both.append(
                jnp.dot(
                    turned_state[head * HD : head * HD + HD, :ROWS],
                    feats[:, lanes],
                    preferred_element_type=jnp.float32,
                )
            )
        result = jnp.concatenate(both, 0) * factor
        out[lanes, :] = result.T.astype(out.dtype)


def in_vmem():
    return pl.BlockSpec(memory_space=pltpu.VMEM)


def make_state(keys, values, rows):
    tokens = keys.shape[0]
    return pl.pallas_call(
        state_kernel,
        out_shape=jax.ShapeDtypeStruct((rows, WIDE), jnp.bfloat16),
        in_specs=[in_vmem(), in_vmem()],
        out_specs=in_vmem(),
        scratch_shapes=[
            pltpu.VMEM((WIDE, tokens), jnp.float32),
            pltpu.VMEM((WIDE, tokens), jnp.bfloat16),
        ],
        compiler_params=pltpu.CompilerParams(vmem_limit_bytes=48 * 2**20),
        name="state",
    )(keys, values)


def read_state(scale, queries, state):
    tokens = queries.shape[0]
    return pl.pallas_call(
        functools.partial(read_kernel, min(512, tokens)),
        out_shape=jax.ShapeDtypeStruct((tokens, WIDE), jnp.bfloat16),
        in_specs=[pl.BlockSpec(memory_space=pltpu.SMEM), in_vmem(), in_vmem()],
        out_specs=in_vmem(),
        scratch_shapes=[
            pltpu.VMEM((WIDE, tokens), jnp.float32),
            pltpu.VMEM((WIDE, tokens), jnp.bfloat16),
            pltpu.VMEM((ROWS, tokens), jnp.bfloat16),
        ],
        compiler_params=pltpu.CompilerParams(vmem_limit_bytes=48 * 2**20),
        name="read",
    )(scale, queries, state)


def on_device(queries, keys, values):
    plane = lax.axis_size(PLANE)
    groups = lax.axis_size(("pair", "core"))
    shards = plane // groups
    part = -(-ROWS // (plane * 8)) * 8
    local = make_state(keys, values, plane * part).reshape(plane, part, WIDE)
    arrived = lax.all_to_all(local, PLANE, 0, 0, tiled=True)
    totals = jnp.sum(arrived.reshape(groups, shards, part, WIDE).astype(jnp.float32), 1)
    whole = jnp.sum(totals, 0)
    layers = lax.axis_size("depth")
    copies = jnp.broadcast_to(whole[None], (layers, part, WIDE))
    others = lax.all_to_all(copies, "depth", 0, 0, tiled=True)
    earlier = jnp.arange(layers) < lax.axis_index("depth")
    before = jnp.sum(jnp.where(earlier[:, None, None], others, 0.0), 0)
    running = []
    for group in range(groups):
        before = before + totals[group]
        running.append(before.astype(jnp.bfloat16))
    inclusive = jnp.stack(running)
    copies = jnp.broadcast_to(inclusive[:, None], (groups, shards, part, WIDE))
    state = lax.all_to_all(copies.reshape(plane, part, WIDE), PLANE, 0, 0, tiled=True)
    count = (lax.axis_index(("depth", "pair", "core")) + 1).astype(jnp.float32)
    scale = 1.0 / (HD * jnp.sqrt(count * (queries.shape[0] * shards)))
    return read_state(scale.reshape(1), queries, state.reshape(plane * part, WIDE))


def solution(mesh):
    torus = Mesh(mesh.devices.reshape(8, 2, 2, 2, 4), EVERY)
    spec = P(EVERY, None)
    return jax.shard_map(
        on_device, mesh=torus, in_specs=(spec, spec, spec), out_specs=spec, check_vma=False
    )
```

time: 145 us -> 71.4 us (0.49)
  the two profiles are of different devices: /device:TPU:2 before, /device:TPU:1 now
where the time goes in v1:
time: 71.4 us; the launch traced here: 71 us
  waiting for transfers between devices  24.3 us (34%)
  blocking collectives  20.4 us (29%)
  starting transfers between devices  13.1 us (18%)
  Pallas kernels  9.04 us (13%)
  local copies, waits for them, and re-layouts  3.71 us (5%)
    all_to_all x1, blocking collectives, on_device(): arrived = lax.all_to_all(local, PLANE, 0, 0, tiled=True)  20.4 us
    all_to_all x1, waiting for transfers between devices, on_device(): others = lax.all_to_all(copies, 'depth', 0, 0, tiled=True)  12.4 us
    all_to_all x1, waiting for transfers between devices, on_device(): lax.all_to_all(copies.reshape(plane, part, WIDE), PLANE, 0, 0, tiled=True)  11.9 us
    all_to_all x1, starting transfers between devices, on_device(): others = lax.all_to_all(copies, 'depth', 0, 0, tiled=True)  8.19 us
    all_to_all x1, starting transfers between devices, on_device(): lax.all_to_all(copies.reshape(plane, part, WIDE), PLANE, 0, 0, tiled=True)  4.95 us
    pallas_call x1, Pallas kernels, make_state(): pl.pallas_call(state_kernel, out_shape=jax.ShapeDtypeStruct((rows, WIDE),...  4.78 us
    pallas_call x1, Pallas kernels, read_state(): pl.pallas_call(functools.partial(read_kernel, min(512, tokens)), out_shap...  4.26 us
    unnamed x6, local copies, waits for them, and re-layouts  2.09 us
  transfers between devices with their start and end apart: 2, of which 2 were waited for; matrix products, arithmetic and copies ran while one was open for 0% of the time, Pallas kernels for 0%

profile of v1, /device:TPU:1, one launch (start us, length us, event | category | flops | bytes accessed | tf_op | source)
XLA Modules:
  0.0 71.0 jit_solution(7532684006897757952)
XLA Ops:
  0.0 0.0 copy-start
  0.0 1.0 %copy-done = bf16[2048,128]{1,0:T(8,128)(2,1)S(1)} copy-done((bf16[2048,128]{1,0:T(8,128)(2,1)S(1)}, bf16[2048,128]{1,0:T(8,128)(2,1)}, u32[]{:S(2)}) %copy-start) | copy-done | bytes 524312
  1.0 0.0 copy-start.1
  1.0 1.0 %copy-done.1 = bf16[2048,128]{1,0:T(8,128)(2,1)S(1)} copy-done((bf16[2048,128]{1,0:T(8,128)(2,1)S(1)}, bf16[2048,128]{1,0:T(8,128)(2,1)}, u32[]{:S(2)}) %copy-start.1) | copy-done | bytes 524312
  2.1 4.8 %state.1 = bf16[2304,128]{1,0:T(8,128)(2,1)S(1)} custom-call(bf16[2048,128]{1,0:T(8,128)(2,1)S(1)} %copy-done, bf16[2048,128]{1,0:T(8,128)(2,1)S(1)} %copy-done.1), custom_call_target="tpu_custom_call" | custom-call | tf_op jit(solution)/shard_map/state/pallas_call | solution.py:101
  6.9 20.4 %all_to_all.15 = bf16[32,72,128]{2,1,0:T(8,128)(2,1)S(1)} all-to-all(bf16[32,72,128]{2,1,0:T(8,128)(2,1)S(1)} %bitcast.13), channel_id=1, replica_groups=mesh['depth'=8,'pair'=2,'core'=2,'near'=2,'row'=4] {'pair','core','near'..., dimensions={0} | all-to-all | bytes 1179648 | tf_op jit(solution)/shard_map/all_to_all | solution.py:138
  27.3 0.1 convert_reduce_fusion
  27.4 0.7 %broadcast_in_dim.26 = f32[8,72,128]{2,1,0:T(8,128)} broadcast(f32[72,128]{1,0:T(8,128)S(1)} %convert_reduce_fusion), dimensions={1,2} | broadcast | bytes 331776 | tf_op jit(solution)/shard_map/broadcast_in_dim | solution.py:142
  28.1 8.2 %all-to-all-start.1 = ((f32[8,72,128]{2,1,0:T(8,128)}), f32[8,72,128]{2,1,0:T(8,128)S(1)}, u32[]{:S(2)}, u32[]{:S(2)}) async-start(f32[8,72,128]{2,1,0:T(8,128)} %broadcast_in_dim.26), calls=%async_computation.1 | async-start | bytes 589824 | tf_op jit(solution)/shard_map/all_to_all | solution.py:143
  36.3 0.1 bitcast_reduce_fusion
  36.4 12.4 %all-to-all-done.1 = f32[8,72,128]{2,1,0:T(8,128)S(1)} async-done(((f32[8,72,128]{2,1,0:T(8,128)}), f32[8,72,128]{2,1,0:T(8,128)S(1)}, u32[]{:S(2)}, u32[]{:S(2)}) %all-to-all-start.1) | async-done | bytes 294944 | tf_op jit(solution)/shard_map/all_to_all | solution.py:143
  48.7 0.1 select_reduce_fusion
  48.9 0.9 %broadcast_in_dim.28 = bf16[4,8,72,128]{3,2,1,0:T(8,128)(2,1)} broadcast(bf16[4,72,128]{2,1,0:T(8,128)(2,1)S(1)} %pad_maximum_fusion), dimensions={0,2,3} | broadcast | bytes 663552 | tf_op jit(solution)/shard_map/broadcast_in_dim | solution.py:151
  49.8 0.0 copy-start.2
  49.8 4.9 %all-to-all-start.2 = ((bf16[32,72,128]{2,1,0:T(8,128)(2,1)}), bf16[32,72,128]{2,1,0:T(8,128)(2,1)S(1)}, u32[]{:S(2)}, u32[]{:S(2)}) async-start(bf16[32,72,128]{2,1,0:T(8,128)(2,1)} %bitcast.4), calls=%async_computation.2 | async-start | bytes 1179648 | tf_op jit(solution)/shard_map/all_to_all | solution.py:152
  54.8 11.9 %all-to-all-done.2 = bf16[32,72,128]{2,1,0:T(8,128)(2,1)S(1)} async-done(((bf16[32,72,128]{2,1,0:T(8,128)(2,1)}), bf16[32,72,128]{2,1,0:T(8,128)(2,1)S(1)}, u32[]{:S(2)}, u32[]{:S(2)}) %all-to-all-start.2) | async-done | bytes 589856 | tf_op jit(solution)/shard_map/all_to_all | solution.py:152
  66.7 0.0 copy-done.2
  66.7 4.3 %read.1 = bf16[2048,128]{1,0:T(8,128)(2,1)} custom-call(f32[1]{0:T(128)} %bitcast.scale, bf16[2048,128]{1,0:T(8,128)(2,1)S(1)} %copy-done.2, bf16[2304,128]{1,0:T(8,128)(2,1)S(1)} %bitcast.14), custom_call_target="tpu_custom_call" | custom-call | tf_op jit(solution)/shard_map/read/pallas_call | solution.py:117
  (4 shorter events, 0.0 us)
Async XLA Ops:
  0.0 1.0 %copy-start = (bf16[2048,128]{1,0:T(8,128)(2,1)S(1)}, bf16[2048,128]{1,0:T(8,128)(2,1)}, u32[]{:S(2)}) copy-start(bf16[2048,128]{1,0:T(8,128)(2,1)} %keys.1) | copy-start | bytes 1572868
  1.0 1.0 %copy-start.1 = (bf16[2048,128]{1,0:T(8,128)(2,1)S(1)}, bf16[2048,128]{1,0:T(8,128)(2,1)}, u32[]{:S(2)}) copy-start(bf16[2048,128]{1,0:T(8,128)(2,1)} %values.1) | copy-start | bytes 1572868
  28.1 20.6 %all-to-all-start.1 = ((f32[8,72,128]{2,1,0:T(8,128)}), f32[8,72,128]{2,1,0:T(8,128)S(1)}, u32[]{:S(2)}, u32[]{:S(2)}) async-start(f32[8,72,128]{2,1,0:T(8,128)} %broadcast_in_dim.26), calls=%async_computation.1 | async-start | bytes 589824 | tf_op jit(solution)/shard_map/all_to_all | solution.py:143
  49.8 17.0 %copy-start.2 = (bf16[2048,128]{1,0:T(8,128)(2,1)S(1)}, bf16[2048,128]{1,0:T(8,128)(2,1)}, u32[]{:S(2)}) copy-start(bf16[2048,128]{1,0:T(8,128)(2,1)} %queries.1) | copy-start | bytes 1572868
  49.8 17.0 %all-to-all-start.2 = ((bf16[32,72,128]{2,1,0:T(8,128)(2,1)}), bf16[32,72,128]{2,1,0:T(8,128)(2,1)S(1)}, u32[]{:S(2)}, u32[]{:S(2)}) async-start(bf16[32,72,128]{2,1,0:T(8,128)(2,1)} %bitcast.4), calls=%async_computation.2 | async-start | bytes 1179648 | tf_op jit(solution)/shard_map/all_to_all | solution.py:152

commit v2 on v1

--- a/solution.py
+++ b/solution.py
@@ -18,6 +18,9 @@
 SAME = [(a, a) for a in range(BLOCKS)]
 ROWS = (HALF + 1) * BLOCK * len(SAME) + BLOCK * BLOCK * len(PAIRS)
 
+CHUNKS = 4
+TILE = 512
+
 PLANE = ("pair", "core", "near", "row")
 EVERY = ("depth",) + PLANE
 
@@ -47,28 +50,52 @@
     return [first[a] * second[b] for a, b in pairs]
 
 
-def state_kernel(keys, values, out, flat, plain):
-    wide = keys[...].astype(jnp.float32).T
-    flat[...] = wide
-    plain[...] = wide.astype(jnp.bfloat16)
-    lanes = pl.ds(0, keys.shape[0])
-    left = lax.broadcasted_iota(jnp.int32, (1, WIDE), 1) < HD
+def state_kernel(keys_far, values_far, out_far, keys, values, flat, plain, out, arrived, left):
+    tokens = keys.shape[0]
+    piece = tokens // CHUNKS
+    loads = []
+    for k in range(CHUNKS):
+        rows = pl.ds(k * piece, piece)
+        loads.append(pltpu.make_async_copy(keys_far.at[rows], keys.at[rows], arrived.at[k]))
+    loads.append(pltpu.make_async_copy(values_far, values, arrived.at[CHUNKS]))
+    for load in loads:
+        load.start()
+    for k in range(CHUNKS):
+        loads[k].wait()
+        rows = pl.ds(k * piece, piece)
+        wide = keys[rows, :].astype(jnp.float32).T
+        flat[:, rows] = wide
+        plain[:, rows] = wide.astype(jnp.bfloat16)
+    loads[CHUNKS].wait()
+    lanes = pl.ds(0, tokens)
+    first_head = lax.broadcasted_iota(jnp.int32, (1, WIDE), 1) < HD
+    stores, sent = [], 0
     for turn, same, pairs, row in pieces():
         count = BLOCK * (len(same) + len(pairs))
         sums = []
         for head in range(HEADS):
             feats = jnp.concatenate(features(flat, plain, head, turn, same + pairs, lanes), 0)
             sums.append(jnp.dot(feats, values[...], preferred_element_type=jnp.float32))
-        total = jnp.where(left, sums[0], sums[1])
+        total = jnp.where(first_head, sums[0], sums[1])
         once = BLOCK * len(same) if turn in (0, HALF) else 0
         if once:
             out[pl.ds(row, once), :] = total[:once].astype(out.dtype)
         out[pl.ds(row + once, count - once), :] = (2.0 * total[once:]).astype(out.dtype)
-    if out.shape[0] > ROWS:
-        out[pl.ds(ROWS, out.shape[0] - ROWS), :] = jnp.zeros((out.shape[0] - ROWS, WIDE), out.dtype)
-
-
-def read_kernel(tile, scale, queries, state, out, flat, plain, feats):
+        done = row + count
+        if turn == BLOCK - 1 and out.shape[0] > ROWS:
+            out[pl.ds(ROWS, out.shape[0] - ROWS), :] = jnp.zeros((out.shape[0] - ROWS, WIDE), out.dtype)
+            done = out.shape[0]
+        if turn % 4 == 3:
+            rows = pl.ds(sent, done - sent)
+            stores.append(pltpu.make_async_copy(out.at[rows], out_far.at[rows], left.at[len(stores)]))
+            stores[-1].start()
+            sent = done
+    for store in stores:
+        store.wait()
+
+
+def read_kernel(tile, scale, queries, state, out_far, out, flat, plain, feats, left):
+    stores = []
     turned_state = state[...].astype(jnp.float32).T.astype(jnp.bfloat16)
     wide = queries[...].astype(jnp.float32).T
     flat[...] = wide
@@ -90,10 +117,18 @@
             )
         result = jnp.concatenate(both, 0) * factor
         out[lanes, :] = result.T.astype(out.dtype)
+        stores.append(pltpu.make_async_copy(out.at[lanes], out_far.at[lanes], left.at[step]))
+        stores[-1].start()
+    for store in stores:
+        store.wait()
 
 
 def in_vmem():
     return pl.BlockSpec(memory_space=pltpu.VMEM)
+
+
+def in_hbm():
+    return pl.BlockSpec(memory_space=pltpu.HBM)
 
 
 def make_state(keys, values, rows):
@@ -101,28 +136,36 @@
     return pl.pallas_call(
         state_kernel,
         out_shape=jax.ShapeDtypeStruct((rows, WIDE), jnp.bfloat16),
-        in_specs=[in_vmem(), in_vmem()],
-        out_specs=in_vmem(),
+        in_specs=[in_hbm(), in_hbm()],
+        out_specs=in_hbm(),
         scratch_shapes=[
+            pltpu.VMEM((tokens, WIDE), jnp.bfloat16),
+            pltpu.VMEM((tokens, WIDE), jnp.bfloat16),
             pltpu.VMEM((WIDE, tokens), jnp.float32),
             pltpu.VMEM((WIDE, tokens), jnp.bfloat16),
+            pltpu.VMEM((rows, WIDE), jnp.bfloat16),
+            pltpu.SemaphoreType.DMA((CHUNKS + 1,)),
+            pltpu.SemaphoreType.DMA((BLOCK // 4,)),
         ],
-        compiler_params=pltpu.CompilerParams(vmem_limit_bytes=48 * 2**20),
+        compiler_params=pltpu.CompilerParams(vmem_limit_bytes=63 * 2**20),
         name="state",
     )(keys, values)
 
 
 def read_state(scale, queries, state):
     tokens = queries.shape[0]
+    tile = min(TILE, tokens)
     return pl.pallas_call(
-        functools.partial(read_kernel, min(512, tokens)),
+        functools.partial(read_kernel, tile),
         out_shape=jax.ShapeDtypeStruct((tokens, WIDE), jnp.bfloat16),
         in_specs=[pl.BlockSpec(memory_space=pltpu.SMEM), in_vmem(), in_vmem()],
-        out_specs=in_vmem(),
+        out_specs=in_hbm(),
         scratch_shapes=[
+            pltpu.VMEM((tokens, WIDE), jnp.bfloat16),
             pltpu.VMEM((WIDE, tokens), jnp.float32),
             pltpu.VMEM((WIDE, tokens), jnp.bfloat16),
             pltpu.VMEM((ROWS, tokens), jnp.bfloat16),
+            pltpu.SemaphoreType.DMA((tokens // tile,)),
         ],
         compiler_params=pltpu.CompilerParams(vmem_limit_bytes=48 * 2**20),
         name="read",
@@ -137,12 +180,12 @@
     local = make_state(keys, values, plane * part).reshape(plane, part, WIDE)
     arrived = lax.all_to_all(local, PLANE, 0, 0, tiled=True)
     totals = jnp.sum(arrived.reshape(groups, shards, part, WIDE).astype(jnp.float32), 1)
-    whole = jnp.sum(totals, 0)
+    whole = jnp.sum(totals, 0).astype(jnp.bfloat16)
     layers = lax.axis_size("depth")
     copies = jnp.broadcast_to(whole[None], (layers, part, WIDE))
     others = lax.all_to_all(copies, "depth", 0, 0, tiled=True)
     earlier = jnp.arange(layers) < lax.axis_index("depth")
-    before = jnp.sum(jnp.where(earlier[:, None, None], others, 0.0), 0)
+    before = jnp.sum(jnp.where(earlier[:, None, None], others.astype(jnp.float32), 0.0), 0)
     running = []
     for group in range(groups):
         before = before + totals[group]

time: 71.4 us -> 68.1 us (0.954)
  waiting for transfers between devices: 24.3 us -> 20.1 us
  local copies, waits for them, and re-layouts: 3.71 us -> 1.57 us
  Pallas kernels: 9.04 us -> 10.9 us
  starting transfers between devices: 13.1 us -> 14.1 us
    all_to_all x1, waiting for transfers between devices: 12.4 us -> 8.23 us  [on_device(): others = lax.all_to_all(copies, 'depth', 0, 0, tiled=True)]
    unnamed x6 -> x2, local copies, waits for them, and re-layouts: 2.09 us -> 0.01 us
    pallas_call x1, Pallas kernels: 4.78 us -> 6.73 us  [make_state(): pl.pallas_call(state_kernel, out_shape=jax.ShapeDtypeStruct((rows, WIDE),...]
    all_to_all x1, starting transfers between devices: 4.95 us -> 5.91 us  [on_device(): lax.all_to_all(copies.reshape(plane, part, WIDE), PLANE, 0, 0, tiled=True)]
where the time goes in v2:
time: 68.1 us; the launch traced here: 67.7 us
  blocking collectives  20.6 us (30%)
  waiting for transfers between devices  20.1 us (30%)
  starting transfers between devices  14.1 us (21%)
  Pallas kernels  10.9 us (16%)
  local copies, waits for them, and re-layouts  1.57 us (2%)
    all_to_all x1, blocking collectives, on_device(): arrived = lax.all_to_all(local, PLANE, 0, 0, tiled=True)  20.6 us
    all_to_all x1, waiting for transfers between devices, on_device(): lax.all_to_all(copies.reshape(plane, part, WIDE), PLANE, 0, 0, tiled=True)  11.9 us
    all_to_all x1, waiting for transfers between devices, on_device(): others = lax.all_to_all(copies, 'depth', 0, 0, tiled=True)  8.23 us
    all_to_all x1, starting transfers between devices, on_device(): others = lax.all_to_all(copies, 'depth', 0, 0, tiled=True)  8.18 us
    pallas_call x1, Pallas kernels, make_state(): pl.pallas_call(state_kernel, out_shape=jax.ShapeDtypeStruct((rows, WIDE),...  6.73 us
    all_to_all x1, starting transfers between devices, on_device(): lax.all_to_all(copies.reshape(plane, part, WIDE), PLANE, 0, 0, tiled=True)  5.91 us
    pallas_call x1, Pallas kernels, read_state(): pl.pallas_call(functools.partial(read_kernel, tile), out_shape=jax.ShapeD...  4.15 us
  transfers between devices with their start and end apart: 2, of which 2 were waited for; matrix products, arithmetic and copies ran while one was open for 0% of the time, Pallas kernels for 0%

profile of v2, /device:TPU:1, one launch (start us, length us, event | category | flops | bytes accessed | tf_op | source)
XLA Modules:
  0.0 67.7 jit_solution(14867178961058484671)
XLA Ops:
  0.0 6.7 %state.1 = bf16[2304,128]{1,0:T(8,128)(2,1)} custom-call(bf16[2048,128]{1,0:T(8,128)(2,1)} %keys_far.1, bf16[2048,128]{1,0:T(8,128)(2,1)} %values_far.1), custom_call_target="tpu_custom_call" | custom-call | tf_op jit(solution)/shard_map/state/pallas_call | solution.py:136
  6.7 20.6 %all_to_all.15 = bf16[32,72,128]{2,1,0:T(8,128)(2,1)S(1)} all-to-all(bf16[32,72,128]{2,1,0:T(8,128)(2,1)} %bitcast.15), channel_id=1, replica_groups=mesh['depth'=8,'pair'=2,'core'=2,'near'=2,'row'=4] {'pair','core','near'..., dimensions={0} | all-to-all | bytes 1179648 | tf_op jit(solution)/shard_map/all_to_all | solution.py:181
  27.3 0.1 reduce_sum.32
  27.4 0.7 %broadcast_in_dim.26 = bf16[8,72,128]{2,1,0:T(8,128)(2,1)} broadcast(bf16[72,128]{1,0:T(8,128)(2,1)S(1)} %reduce_sum.32), dimensions={1,2} | broadcast | bytes 165888 | tf_op jit(solution)/shard_map/broadcast_in_dim | solution.py:185
  28.1 8.2 %all-to-all-start.1 = ((bf16[8,72,128]{2,1,0:T(8,128)(2,1)}), bf16[8,72,128]{2,1,0:T(8,128)(2,1)S(1)}, u32[]{:S(2)}, u32[]{:S(2)}) async-start(bf16[8,72,128]{2,1,0:T(8,128)(2,1)} %broadcast_in_dim.26), calls=%async_computation.1 | async-start | bytes 294912 | tf_op jit(solution)/shard_map/all_to_all | solution.py:186
  36.3 0.1 convert_reduce_fusion
  36.4 8.2 %all-to-all-done.1 = bf16[8,72,128]{2,1,0:T(8,128)(2,1)S(1)} async-done(((bf16[8,72,128]{2,1,0:T(8,128)(2,1)}), bf16[8,72,128]{2,1,0:T(8,128)(2,1)S(1)}, u32[]{:S(2)}, u32[]{:S(2)}) %all-to-all-start.1) | async-done | bytes 147488 | tf_op jit(solution)/shard_map/all_to_all | solution.py:186
  44.6 0.1 select_reduce_fusion
  44.8 0.9 %broadcast_in_dim.28 = bf16[4,8,72,128]{3,2,1,0:T(8,128)(2,1)} broadcast(bf16[4,72,128]{2,1,0:T(8,128)(2,1)S(1)} %pad_maximum_fusion), dimensions={0,2,3} | broadcast | bytes 663552 | tf_op jit(solution)/shard_map/broadcast_in_dim | solution.py:194
  45.7 0.0 copy-start
  45.7 5.9 %all-to-all-start.2 = ((bf16[32,72,128]{2,1,0:T(8,128)(2,1)}), bf16[32,72,128]{2,1,0:T(8,128)(2,1)S(1)}, u32[]{:S(2)}, u32[]{:S(2)}) async-start(bf16[32,72,128]{2,1,0:T(8,128)(2,1)} %bitcast.4), calls=%async_computation.2 | async-start | bytes 1179648 | tf_op jit(solution)/shard_map/all_to_all | solution.py:195
  51.7 11.9 %all-to-all-done.2 = bf16[32,72,128]{2,1,0:T(8,128)(2,1)S(1)} async-done(((bf16[32,72,128]{2,1,0:T(8,128)(2,1)}), bf16[32,72,128]{2,1,0:T(8,128)(2,1)S(1)}, u32[]{:S(2)}, u32[]{:S(2)}) %all-to-all-start.2) | async-done | bytes 589856 | tf_op jit(solution)/shard_map/all_to_all | solution.py:195
  63.6 0.0 copy-done
  63.6 4.1 %read.1 = bf16[2048,128]{1,0:T(8,128)(2,1)} custom-call(f32[1]{0:T(128)} %bitcast.scale, bf16[2048,128]{1,0:T(8,128)(2,1)S(1)} %copy-done, bf16[2304,128]{1,0:T(8,128)(2,1)S(1)} %bitcast.14), custom_call_target="tpu_custom_call" | custom-call | tf_op jit(solution)/shard_map/read/pallas_call | solution.py:158
  (4 shorter events, 0.0 us)
Async XLA Ops:
  28.1 16.5 %all-to-all-start.1 = ((bf16[8,72,128]{2,1,0:T(8,128)(2,1)}), bf16[8,72,128]{2,1,0:T(8,128)(2,1)S(1)}, u32[]{:S(2)}, u32[]{:S(2)}) async-start(bf16[8,72,128]{2,1,0:T(8,128)(2,1)} %broadcast_in_dim.26), calls=%async_computation.1 | async-start | bytes 294912 | tf_op jit(solution)/shard_map/all_to_all | solution.py:186
  45.7 17.9 %copy-start = (bf16[2048,128]{1,0:T(8,128)(2,1)S(1)}, bf16[2048,128]{1,0:T(8,128)(2,1)}, u32[]{:S(2)}) copy-start(bf16[2048,128]{1,0:T(8,128)(2,1)} %queries.1) | copy-start | bytes 1572868
  45.7 17.9 %all-to-all-start.2 = ((bf16[32,72,128]{2,1,0:T(8,128)(2,1)}), bf16[32,72,128]{2,1,0:T(8,128)(2,1)S(1)}, u32[]{:S(2)}, u32[]{:S(2)}) async-start(bf16[32,72,128]{2,1,0:T(8,128)(2,1)} %bitcast.4), calls=%async_computation.2 | async-start | bytes 1179648 | tf_op jit(solution)/shard_map/all_to_all | solution.py:195

commit v3 on v2

v3 whole, which is shorter than its diff:
```python
import functools

import jax
import jax.numpy as jnp
from jax import lax
from jax.experimental import pallas as pl
from jax.experimental.pallas import tpu as pltpu
from jax.sharding import Mesh
from jax.sharding import PartitionSpec as P

HD = 64
HEADS = 2
WIDE = HEADS * HD
BLOCK = 16
BAND = 2 * HD
ROWS = BLOCK * BAND + HD
CHUNK = 1024
TILE = 2048

PLANE = ("pair", "core", "near", "row")
EVERY = ("depth",) + PLANE


def band(flat, plain, head, s, lanes):
    rows = pl.ds(head * HD, HD)
    x = plain[rows, lanes]
    blocks = [plain[pl.ds(head * HD + k * BLOCK, BLOCK), lanes] for k in range(HD // BLOCK)]
    if s == BLOCK:
        return x * jnp.concatenate(blocks[2:] + blocks[:2], 0)
    lifted = jnp.concatenate(blocks[-1:] + blocks[:-1], 0)
    other = x
    if s:
        other = pltpu.roll(flat[rows, lanes], HD - s, 0).astype(jnp.bfloat16)
    return jnp.concatenate([x * other, lifted * other], 0)


def state_kernel(keys_far, values_far, out_far, keys, values, flat, plain, total, out, arrived, left):
    tokens = keys.shape[0]
    loads = []
    for k in range(tokens // CHUNK):
        rows = pl.ds(k * CHUNK, CHUNK)
        loads.append(pltpu.make_async_copy(keys_far.at[rows], keys.at[rows], arrived.at[2 * k]))
        loads.append(pltpu.make_async_copy(values_far.at[rows], values.at[rows], arrived.at[2 * k + 1]))
    for load in loads:
        load.start()
    padding = out.shape[0] - ROWS
    out[pl.ds(ROWS, padding), :] = jnp.zeros((padding, WIDE), out.dtype)
    first_head = lax.broadcasted_iota(jnp.int32, (1, WIDE), 1) < HD
    row = lax.broadcasted_iota(jnp.int32, (BAND, 1), 0)
    stores, sent = [], 0
    for k in range(tokens // CHUNK):
        last = k == tokens // CHUNK - 1
        lanes = pl.ds(k * CHUNK, CHUNK)
        loads[2 * k].wait()
        wide = keys[lanes, :].astype(jnp.float32).T
        flat[:, lanes] = wide
        plain[:, lanes] = wide.astype(jnp.bfloat16)
        loads[2 * k + 1].wait()
        for s in range(BLOCK + 1):
            sums = []
            for head in range(HEADS):
                feats = band(flat, plain, head, s, lanes)
                sums.append(jnp.dot(feats, values[lanes, :], preferred_element_type=jnp.float32))
            product = jnp.where(first_head, sums[0], sums[1])
            here = pl.ds(s * BAND, product.shape[0])
            if k:
                product = product + total[here, :]
            if not last:
                total[here, :] = product
                continue
            if s == 0:
                product = product * jnp.where(row < HD, 1.0, 2.0)
            elif s < BLOCK:
                product = product * 2.0
            out[here, :] = product.astype(out.dtype)
            if s % 4 == 3 or s == BLOCK:
                done = out.shape[0] if s == BLOCK else (s + 1) * BAND
                rows = pl.ds(sent, done - sent)
                stores.append(pltpu.make_async_copy(out.at[rows], out_far.at[rows], left.at[len(stores)]))
                stores[-1].start()
                sent = done
    for store in stores:
        store.wait()


def read_kernel(scale, queries, state, out_far, out, flat, plain, feats, left):
    turned = state[...].astype(jnp.float32).T.astype(jnp.bfloat16)
    wide = queries[...].astype(jnp.float32).T
    flat[...] = wide
    plain[...] = wide.astype(jnp.bfloat16)
    factor = scale[0]
    stores = []
    for step in range(out.shape[0] // TILE):
        lanes = pl.ds(step * TILE, TILE)
        both = []
        for head in range(HEADS):
            here = turned[head * HD : head * HD + HD, :ROWS]
            product = jnp.zeros((HD, TILE), jnp.float32)
            begin = 0
            for s in range(BLOCK + 1):
                value = band(flat, plain, head, s, lanes)
                feats[head, pl.ds(s * BAND, value.shape[0]), lanes] = value
                if s == BLOCK or s % 2 == 1 and s < BLOCK - 1:
                    end = s * BAND + value.shape[0]
                    product += jnp.dot(
                        here[:, begin:end],
                        feats[head, pl.ds(begin, end - begin), lanes],
                        preferred_element_type=jnp.float32,
                    )
                    begin = end
            both.append(product)
        result = jnp.concatenate(both, 0) * factor
        out[lanes, :] = result.T.astype(out.dtype)
        stores.append(pltpu.make_async_copy(out.at[lanes], out_far.at[lanes], left.at[step]))
        stores[-1].start()
    for store in stores:
        store.wait()


def in_vmem():
    return pl.BlockSpec(memory_space=pltpu.VMEM)


def in_hbm():
    return pl.BlockSpec(memory_space=pltpu.HBM)


def make_state(keys, values, rows):
    tokens = keys.shape[0]
    return pl.pallas_call(
        state_kernel,
        out_shape=jax.ShapeDtypeStruct((rows, WIDE), jnp.bfloat16),
        in_specs=[in_hbm(), in_hbm()],
        out_specs=in_hbm(),
        scratch_shapes=[
            pltpu.VMEM((tokens, WIDE), jnp.bfloat16),
            pltpu.VMEM((tokens, WIDE), jnp.bfloat16),
            pltpu.VMEM((WIDE, tokens), jnp.float32),
            pltpu.VMEM((WIDE, tokens), jnp.bfloat16),
            pltpu.VMEM((ROWS, WIDE), jnp.float32),
            pltpu.VMEM((rows, WIDE), jnp.bfloat16),
            pltpu.SemaphoreType.DMA((2 * tokens // CHUNK,)),
            pltpu.SemaphoreType.DMA((BLOCK // 4 + 1,)),
        ],
        compiler_params=pltpu.CompilerParams(vmem_limit_bytes=62 * 2**20),
        name="state",
    )(keys, values)


def read_state(scale, queries, state):
    tokens = queries.shape[0]
    return pl.pallas_call(
        read_kernel,
        out_shape=jax.ShapeDtypeStruct((tokens, WIDE), jnp.bfloat16),
        in_specs=[pl.BlockSpec(memory_space=pltpu.SMEM), in_vmem(), in_vmem()],
        out_specs=in_hbm(),
        scratch_shapes=[
            pltpu.VMEM((tokens, WIDE), jnp.bfloat16),
            pltpu.VMEM((WIDE, tokens), jnp.float32),
            pltpu.VMEM((WIDE, tokens), jnp.bfloat16),
            pltpu.VMEM((HEADS, ROWS, tokens), jnp.bfloat16),
            pltpu.SemaphoreType.DMA((tokens // TILE,)),
        ],
        compiler_params=pltpu.CompilerParams(vmem_limit_bytes=48 * 2**20),
        name="read",
    )(scale, queries, state)


def on_device(queries, keys, values):
    plane = lax.axis_size(PLANE)
    groups = lax.axis_size(("pair", "core"))
    shards = plane // groups
    part = (-(-ROWS // (plane * 8)) * 8, WIDE)
    local = make_state(keys, values, plane * part[0]).reshape(plane, *part)
    arrived = lax.all_to_all(local, PLANE, 0, 0, tiled=True)
    totals = jnp.sum(arrived.reshape(groups, shards, *part).astype(jnp.float32), 1)
    whole = jnp.sum(totals, 0).astype(jnp.bfloat16)
    layers = lax.axis_size("depth")
    copies = jnp.broadcast_to(whole[None], (layers, *part))
    others = lax.all_to_all(copies, "depth", 0, 0, tiled=True)
    earlier = jnp.arange(layers) < lax.axis_index("depth")
    before = jnp.sum(jnp.where(earlier[:, None, None], others.astype(jnp.float32), 0.0), 0)
    running = []
    for group in range(groups):
        before = before + totals[group]
        running.append(before.astype(jnp.bfloat16))
    inclusive = jnp.stack(running)
    copies = jnp.broadcast_to(inclusive[:, None], (groups, shards, *part))
    state = lax.all_to_all(copies.reshape(plane, *part), PLANE, 0, 0, tiled=True)
    count = (lax.axis_index(("depth", "pair", "core")) + 1).astype(jnp.float32)
    scale = 1.0 / (HD * jnp.sqrt(count * (queries.shape[0] * shards)))
    return read_state(scale.reshape(1), queries, state.reshape(-1, WIDE))


def solution(mesh):
    torus = Mesh(mesh.devices.reshape(8, 2, 2, 2, 4), EVERY)
    spec = P(EVERY, None)
    return jax.shard_map(
        on_device, mesh=torus, in_specs=(spec, spec, spec), out_specs=spec, check_vma=False
    )
```

time: 68.1 us -> 68.2 us (level)
  no operation moved by 1% of the time
where the time goes in v3:
time: 68.2 us; the launch traced here: 67.8 us
  blocking collectives  20.6 us (30%)
  waiting for transfers between devices  20.1 us (29%)
  starting transfers between devices  14.1 us (21%)
  Pallas kernels  10.9 us (16%)
  local copies, waits for them, and re-layouts  1.57 us (2%)
    all_to_all x1, blocking collectives, on_device(): arrived = lax.all_to_all(local, PLANE, 0, 0, tiled=True)  20.6 us
    all_to_all x1, waiting for transfers between devices, on_device(): lax.all_to_all(copies.reshape(plane, *part), PLANE, 0, 0, tiled=True)  11.9 us
    all_to_all x1, waiting for transfers between devices, on_device(): others = lax.all_to_all(copies, 'depth', 0, 0, tiled=True)  8.23 us
    all_to_all x1, starting transfers between devices, on_device(): others = lax.all_to_all(copies, 'depth', 0, 0, tiled=True)  8.19 us
    pallas_call x1, Pallas kernels, make_state(): pl.pallas_call(state_kernel, out_shape=jax.ShapeDtypeStruct((rows, WIDE),...  6.78 us
    all_to_all x1, starting transfers between devices, on_device(): lax.all_to_all(copies.reshape(plane, *part), PLANE, 0, 0, tiled=True)  5.91 us
    pallas_call x1, Pallas kernels, read_state(): pl.pallas_call(read_kernel, out_shape=jax.ShapeDtypeStruct((tokens, WIDE)...  4.15 us
  transfers between devices with their start and end apart: 2, of which 2 were waited for; matrix products, arithmetic and copies ran while one was open for 0% of the time, Pallas kernels for 0%

profile of v3, /device:TPU:1, one launch (start us, length us, event | category | flops | bytes accessed | tf_op | source)
XLA Modules:
  0.0 67.8 jit_solution(13298820911071580140)
XLA Ops:
  0.0 6.8 %state.1 = bf16[2304,128]{1,0:T(8,128)(2,1)} custom-call(bf16[2048,128]{1,0:T(8,128)(2,1)} %keys_far.1, bf16[2048,128]{1,0:T(8,128)(2,1)} %values_far.1), custom_call_target="tpu_custom_call" | custom-call | tf_op jit(solution)/shard_map/state/pallas_call | solution.py:130
  6.8 20.6 %all_to_all.15 = bf16[32,72,128]{2,1,0:T(8,128)(2,1)S(1)} all-to-all(bf16[32,72,128]{2,1,0:T(8,128)(2,1)} %bitcast.15), channel_id=1, replica_groups=mesh['depth'=8,'pair'=2,'core'=2,'near'=2,'row'=4] {'pair','core','near'..., dimensions={0} | all-to-all | bytes 1179648 | tf_op jit(solution)/shard_map/all_to_all | solution.py:175
  27.4 0.1 reduce_sum.32
  27.5 0.7 %broadcast_in_dim.26 = bf16[8,72,128]{2,1,0:T(8,128)(2,1)} broadcast(bf16[72,128]{1,0:T(8,128)(2,1)S(1)} %reduce_sum.32), dimensions={1,2} | broadcast | bytes 165888 | tf_op jit(solution)/shard_map/broadcast_in_dim | solution.py:179
  28.2 8.2 %all-to-all-start.1 = ((bf16[8,72,128]{2,1,0:T(8,128)(2,1)}), bf16[8,72,128]{2,1,0:T(8,128)(2,1)S(1)}, u32[]{:S(2)}, u32[]{:S(2)}) async-start(bf16[8,72,128]{2,1,0:T(8,128)(2,1)} %broadcast_in_dim.26), calls=%async_computation.1 | async-start | bytes 294912 | tf_op jit(solution)/shard_map/all_to_all | solution.py:180
  36.4 0.1 convert_reduce_fusion
  36.4 8.2 %all-to-all-done.1 = bf16[8,72,128]{2,1,0:T(8,128)(2,1)S(1)} async-done(((bf16[8,72,128]{2,1,0:T(8,128)(2,1)}), bf16[8,72,128]{2,1,0:T(8,128)(2,1)S(1)}, u32[]{:S(2)}, u32[]{:S(2)}) %all-to-all-start.1) | async-done | bytes 147488 | tf_op jit(solution)/shard_map/all_to_all | solution.py:180
  44.7 0.1 select_reduce_fusion
  44.8 0.9 %broadcast_in_dim.28 = bf16[4,8,72,128]{3,2,1,0:T(8,128)(2,1)} broadcast(bf16[4,72,128]{2,1,0:T(8,128)(2,1)S(1)} %pad_maximum_fusion), dimensions={0,2,3} | broadcast | bytes 663552 | tf_op jit(solution)/shard_map/broadcast_in_dim | solution.py:188
  45.7 0.0 copy-start
  45.7 5.9 %all-to-all-start.2 = ((bf16[32,72,128]{2,1,0:T(8,128)(2,1)}), bf16[32,72,128]{2,1,0:T(8,128)(2,1)S(1)}, u32[]{:S(2)}, u32[]{:S(2)}) async-start(bf16[32,72,128]{2,1,0:T(8,128)(2,1)} %bitcast.4), calls=%async_computation.2 | async-start | bytes 1179648 | tf_op jit(solution)/shard_map/all_to_all | solution.py:189
  51.7 11.9 %all-to-all-done.2 = bf16[32,72,128]{2,1,0:T(8,128)(2,1)S(1)} async-done(((bf16[32,72,128]{2,1,0:T(8,128)(2,1)}), bf16[32,72,128]{2,1,0:T(8,128)(2,1)S(1)}, u32[]{:S(2)}, u32[]{:S(2)}) %all-to-all-start.2) | async-done | bytes 589856 | tf_op jit(solution)/shard_map/all_to_all | solution.py:189
  63.6 0.0 copy-done
  63.6 4.1 %read.1 = bf16[2048,128]{1,0:T(8,128)(2,1)} custom-call(f32[1]{0:T(128)} %bitcast.scale, bf16[2048,128]{1,0:T(8,128)(2,1)S(1)} %copy-done, bf16[2304,128]{1,0:T(8,128)(2,1)S(1)} %bitcast.14), custom_call_target="tpu_custom_call" | custom-call | tf_op jit(solution)/shard_map/read/pallas_call | solution.py:152
  (4 shorter events, 0.0 us)
Async XLA Ops:
  28.2 16.5 %all-to-all-start.1 = ((bf16[8,72,128]{2,1,0:T(8,128)(2,1)}), bf16[8,72,128]{2,1,0:T(8,128)(2,1)S(1)}, u32[]{:S(2)}, u32[]{:S(2)}) async-start(bf16[8,72,128]{2,1,0:T(8,128)(2,1)} %broadcast_in_dim.26), calls=%async_computation.1 | async-start | bytes 294912 | tf_op jit(solution)/shard_map/all_to_all | solution.py:180
  45.7 17.9 %copy-start = (bf16[2048,128]{1,0:T(8,128)(2,1)S(1)}, bf16[2048,128]{1,0:T(8,128)(2,1)}, u32[]{:S(2)}) copy-start(bf16[2048,128]{1,0:T(8,128)(2,1)} %queries.1) | copy-start | bytes 1572868
  45.7 17.9 %all-to-all-start.2 = ((bf16[32,72,128]{2,1,0:T(8,128)(2,1)}), bf16[32,72,128]{2,1,0:T(8,128)(2,1)S(1)}, u32[]{:S(2)}, u32[]{:S(2)}) async-start(bf16[32,72,128]{2,1,0:T(8,128)(2,1)} %bitcast.4), calls=%async_computation.2 | async-start | bytes 1179648 | tf_op jit(solution)/shard_map/all_to_all | solution.py:189

commit v4 on v3

--- a/solution.py
+++ b/solution.py
@@ -170,26 +170,30 @@
     plane = lax.axis_size(PLANE)
     groups = lax.axis_size(("pair", "core"))
     shards = plane // groups
+    layers = lax.axis_size("depth")
     part = (-(-ROWS // (plane * 8)) * 8, WIDE)
+    count = (lax.axis_index(("depth", "pair", "core")) + 1).astype(jnp.float32)
+    scale = (1.0 / (HD * jnp.sqrt(count * (queries.shape[0] * shards)))).reshape(1)
+    earlier = (jnp.arange(layers) < lax.axis_index("depth")).astype(jnp.float32)
     local = make_state(keys, values, plane * part[0]).reshape(plane, *part)
+    local, earlier, scale = lax.optimization_barrier((local, earlier, scale))
     arrived = lax.all_to_all(local, PLANE, 0, 0, tiled=True)
     totals = jnp.sum(arrived.reshape(groups, shards, *part).astype(jnp.float32), 1)
     whole = jnp.sum(totals, 0).astype(jnp.bfloat16)
-    layers = lax.axis_size("depth")
     copies = jnp.broadcast_to(whole[None], (layers, *part))
+    copies, totals, earlier, scale = lax.optimization_barrier((copies, totals, earlier, scale))
     others = lax.all_to_all(copies, "depth", 0, 0, tiled=True)
-    earlier = jnp.arange(layers) < lax.axis_index("depth")
-    before = jnp.sum(jnp.where(earlier[:, None, None], others.astype(jnp.float32), 0.0), 0)
+    before = jnp.sum(others.astype(jnp.float32) * earlier[:, None, None], 0)
     running = []
     for group in range(groups):
         before = before + totals[group]
         running.append(before.astype(jnp.bfloat16))
     inclusive = jnp.stack(running)
     copies = jnp.broadcast_to(inclusive[:, None], (groups, shards, *part))
-    state = lax.all_to_all(copies.reshape(plane, *part), PLANE, 0, 0, tiled=True)
-    count = (lax.axis_index(("depth", "pair", "core")) + 1).astype(jnp.float32)
-    scale = 1.0 / (HD * jnp.sqrt(count * (queries.shape[0] * shards)))
-    return read_state(scale.reshape(1), queries, state.reshape(-1, WIDE))
+    copies, scale = lax.optimization_barrier((copies.reshape(plane, *part), scale))
+    state = lax.all_to_all(copies, PLANE, 0, 0, tiled=True)
+    state, scale = lax.optimization_barrier((state, scale))
+    return read_state(scale, queries, state.reshape(-1, WIDE))
 
 
 def solution(mesh):

time: 68.2 us -> 66.4 us (0.974)
  blocking collectives: 20.6 us -> 54.6 us
  waiting for transfers between devices: 20.1 us -> 0 us
  starting transfers between devices: 14.1 us -> 0 us
  local copies, waits for them, and re-layouts: 1.57 us -> 0.11 us
    all_to_all x0 -> x2, blocking collectives: none -> 34 us  [the longest x1 17.7 us: on_device(): state = lax.all_to_all(copies, PLANE, 0, 0, tiled=True)]
    all_to_all x2 -> x0, waiting for transfers between devices: 20.1 us -> none  [the longest x1 11.9 us: on_device(): lax.all_to_all(copies.reshape(plane, *part), PLANE, 0, 0, tiled=True)]
    all_to_all x2 -> x0, starting transfers between devices: 14.1 us -> none  [the longest x1 8.19 us: on_device(): others = lax.all_to_all(copies, 'depth', 0, 0, tiled=True)]
    broadcast_in_dim x1, local copies, waits for them, and re-layouts: 0.88 us -> 0.08 us  [on_device(): copies = jnp.broadcast_to(inclusive[:, None], (groups, shards, *part))]
  transfers between devices with their start and end apart: 2 -> 0, of which waited for: 2 -> 0; matrix products, arithmetic and copies ran while one was open for 0% -> 0% of each run, Pallas kernels for 0% -> 0%
where the time goes in v4:
time: 66.4 us; the launch traced here: 66.1 us
  blocking collectives  54.6 us (82%)
  Pallas kernels  10.9 us (16%)
    all_to_all x1, blocking collectives, on_device(): arrived = lax.all_to_all(local, PLANE, 0, 0, tiled=True)  20.6 us
    all_to_all x1, blocking collectives, on_device(): state = lax.all_to_all(copies, PLANE, 0, 0, tiled=True)  17.7 us
    all_to_all x1, blocking collectives, on_device(): others = lax.all_to_all(copies, 'depth', 0, 0, tiled=True)  16.3 us
    pallas_call x1, Pallas kernels, make_state(): pl.pallas_call(state_kernel, out_shape=jax.ShapeDtypeStruct((rows, WIDE),...  6.78 us
    pallas_call x1, Pallas kernels, read_state(): pl.pallas_call(read_kernel, out_shape=jax.ShapeDtypeStruct((tokens, WIDE)...  4.16 us

profile of v4, /device:TPU:1, one launch (start us, length us, event | category | flops | bytes accessed | tf_op | source)
XLA Modules:
  0.0 66.1 jit_solution(4706927602690677769)
XLA Ops:
  0.1 6.8 %state.1 = bf16[2304,128]{1,0:T(8,128)(2,1)} custom-call(bf16[2048,128]{1,0:T(8,128)(2,1)} %keys_far.1, bf16[2048,128]{1,0:T(8,128)(2,1)} %values_far.1), custom_call_target="tpu_custom_call" | custom-call | tf_op jit(solution)/shard_map/state/pallas_call | solution.py:130
  6.9 20.6 %all_to_all.15 = bf16[32,72,128]{2,1,0:T(8,128)(2,1)S(1)} all-to-all(bf16[32,72,128]{2,1,0:T(8,128)(2,1)} %bitcast.11), channel_id=1, replica_groups=mesh['depth'=8,'pair'=2,'core'=2,'near'=2,'row'=4] {'pair','core','near'..., dimensions={0} | all-to-all | bytes 1179648 | tf_op jit(solution)/shard_map/all_to_all | solution.py:180
  27.5 0.1 convert_reduce_fusion
  27.6 0.1 reduce_sum.32
  27.7 16.3 %all_to_all.16 = bf16[8,72,128]{2,1,0:T(8,128)(2,1)S(1)} all-to-all(bf16[8,72,128]{2,1,0:T(8,128)(2,1)S(1)} %broadcast_in_dim.4), channel_id=1, replica_groups=mesh['depth'=8,'pair'=2,'core'=2,'near'=2,'row'=4] {'depth'}, dimensions={0} | all-to-all | bytes 294912 | tf_op jit(solution)/shard_map/all_to_all | solution.py:185
  44.0 0.1 multiply_reduce_fusion
  44.2 0.1 broadcast_in_dim.5
  44.2 0.0 copy-start
  44.3 17.7 %all_to_all.17 = bf16[32,72,128]{2,1,0:T(8,128)(2,1)S(1)} all-to-all(bf16[32,72,128]{2,1,0:T(8,128)(2,1)S(1)} %bitcast.12), channel_id=1, replica_groups=mesh['depth'=8,'pair'=2,'core'=2,'near'=2,'row'=4] {'pair','core','near'..., dimensions={0} | all-to-all | bytes 1179648 | tf_op jit(solution)/shard_map/all_to_all | solution.py:194
  62.0 0.0 copy-done
  62.0 4.2 %read.1 = bf16[2048,128]{1,0:T(8,128)(2,1)} custom-call(f32[1]{0:T(128)} %bitcast.1.scale, bf16[2048,128]{1,0:T(8,128)(2,1)S(1)} %copy-done, bf16[2304,128]{1,0:T(8,128)(2,1)S(1)} %bitcast.10), custom_call_target="tpu_custom_call" | custom-call | tf_op jit(solution)/shard_map/read/pallas_call | solution.py:152
  (5 shorter events, 0.1 us)
Async XLA Ops:
  44.2 17.7 %copy-start = (bf16[2048,128]{1,0:T(8,128)(2,1)S(1)}, bf16[2048,128]{1,0:T(8,128)(2,1)}, u32[]{:S(2)}) copy-start(bf16[2048,128]{1,0:T(8,128)(2,1)} %queries.1) | copy-start | bytes 1572868

commit v5 on v4

v5 whole, which is shorter than its diff:
```python
import jax
import jax.numpy as jnp
import numpy as np
from jax import lax
from jax.experimental import pallas as pl
from jax.experimental.pallas import tpu as pltpu
from jax.sharding import Mesh
from jax.sharding import PartitionSpec as P

HD = 64
HEADS = 2
WIDE = HEADS * HD
BLOCK = 16
BLOCKS = HD // BLOCK
BAND = 2 * HD
ROWS = BLOCK * BAND + HD
STRIP = 9
STRIPS = 4
TALL = 8
PARTS = STRIPS * HD // TALL

DEPTH = ("depth_0", "depth_1", "depth_2")
PLANE = ("pair", "core", "near", "row")
EVERY = DEPTH + PLANE


def head_blocks(wide, step):
    rows = [HD * head + BLOCK * ((k + step) % BLOCKS) for head in range(HEADS) for k in range(BLOCKS)]
    return jnp.concatenate([wide[row : row + BLOCK] for row in rows], 0)


def state_kernel(keys_far, values_far, out_far, keys, values, out, arrived, left):
    loads = [
        pltpu.make_async_copy(keys_far, keys, arrived.at[0]),
        pltpu.make_async_copy(values_far, values, arrived.at[1]),
    ]
    for load in loads:
        load.start()
    filled = (2 * BLOCK + 1) % STRIP * WIDE
    for k in range(HD // TALL):
        rest = out.shape[2] - filled
        out[PARTS - HD // TALL + k, :, pl.ds(filled, rest)] = jnp.zeros((TALL, rest), out.dtype)
    loads[0].wait()
    x = keys[...]
    wide = x.astype(jnp.float32).T
    lifted = head_blocks(wide, -1).astype(jnp.bfloat16).T
    loads[1].wait()
    turned_values = values[...].astype(jnp.float32).T.astype(jnp.bfloat16)
    lane = lax.broadcasted_iota(jnp.int32, (1, WIDE), 1)
    stores = []
    for s in range(BLOCK + 1):
        if s == 0:
            other = x
        elif s == BLOCK:
            other = head_blocks(wide, 2).astype(jnp.bfloat16).T
        else:
            heads = [pltpu.roll(wide[HD * head : HD * head + HD], HD - s, 0) for head in range(HEADS)]
            other = jnp.concatenate(heads, 0).astype(jnp.bfloat16).T
        feats = x * other if s == BLOCK else jnp.concatenate([x * other, lifted * other], 1)
        product = jnp.dot(turned_values, feats, preferred_element_type=jnp.float32)
        for half in range(feats.shape[1] // WIDE):
            piece = product[:, WIDE * half : WIDE * half + WIDE]
            piece = jnp.where(lane < HD, piece[:HD], piece[HD:])
            if s < BLOCK and (s or half):
                piece = 2.0 * piece
            strip, place = divmod(2 * s + half, STRIP)
            for k in range(HD // TALL):
                part = piece[TALL * k : TALL * k + TALL].astype(out.dtype)
                out[HD // TALL * strip + k, :, pl.ds(WIDE * place, WIDE)] = part
            if place == STRIP - 1 or s == BLOCK:
                parts = pl.ds(HD // TALL * strip, HD // TALL)
                stores.append(pltpu.make_async_copy(out.at[parts], out_far.at[parts], left.at[strip]))
                stores[-1].start()
    for store in stores:
        store.wait()


def band(flat, plain, head, s):
    x = plain[pl.ds(head * HD, HD), :]
    blocks = [plain[pl.ds(head * HD + k * BLOCK, BLOCK), :] for k in range(BLOCKS)]
    if s == BLOCK:
        return x * jnp.concatenate(blocks[2:] + blocks[:2], 0)
    lifted = jnp.concatenate(blocks[-1:] + blocks[:-1], 0)
    other = x
    if s:
        other = pltpu.roll(flat[pl.ds(head * HD, HD), :], HD - s, 0).astype(jnp.bfloat16)
    return jnp.concatenate([x * other, lifted * other], 0)


def state_band(whole, head, s):
    lane = lax.broadcasted_iota(jnp.int32, (1, WIDE), 1)
    low = whole[:, pl.ds(2 * s * WIDE, WIDE)]
    if head == 1:
        low = pltpu.roll(low, HD, 1)
    if s == BLOCK:
        return low[:, :HD].astype(jnp.bfloat16)
    high = whole[:, pl.ds(2 * s * WIDE + WIDE, WIDE)]
    if head == 0:
        high = pltpu.roll(high, HD, 1)
    return jnp.where(lane < HD, low, high).astype(jnp.bfloat16)


def read_kernel(scale, queries, state, out, flat, plain, feats, whole):
    for k in range(PARTS):
        strip, rows = divmod(k, HD // TALL)
        lanes = pl.ds(STRIP * WIDE * strip, STRIP * WIDE)
        whole[pl.ds(TALL * rows, TALL), lanes] = state[k].astype(jnp.float32)
    wide = queries[...].astype(jnp.float32).T
    flat[...] = wide
    plain[...] = wide.astype(jnp.bfloat16)
    both = []
    for head in range(HEADS):
        product = jnp.zeros((HD, queries.shape[0]), jnp.float32)
        begin, left = 0, []
        for s in range(BLOCK + 1):
            value = band(flat, plain, head, s)
            end = s * BAND + value.shape[0]
            feats[head, pl.ds(s * BAND, value.shape[0]), :] = value
            left.append(state_band(whole, head, s))
            if s == BLOCK or s % 2 == 1 and s < BLOCK - 1:
                right = feats[head, pl.ds(begin, end - begin), :]
                product += jnp.dot(jnp.concatenate(left, 1), right, preferred_element_type=jnp.float32)
                begin, left = end, []
        both.append(product)
    result = jnp.concatenate(both, 0) * scale[0]
    out[...] = result.T.astype(out.dtype)


def in_vmem():
    return pl.BlockSpec(memory_space=pltpu.VMEM)


def in_hbm():
    return pl.BlockSpec(memory_space=pltpu.HBM)


def make_state(keys, values):
    tokens = keys.shape[0]
    part = (TALL, STRIP * WIDE)
    return pl.pallas_call(
        state_kernel,
        out_shape=jax.ShapeDtypeStruct((PARTS, *part), jnp.bfloat16),
        in_specs=[in_hbm(), in_hbm()],
        out_specs=in_hbm(),
        scratch_shapes=[
            pltpu.VMEM((tokens, WIDE), jnp.bfloat16),
            pltpu.VMEM((tokens, WIDE), jnp.bfloat16),
            pltpu.VMEM((PARTS, *part), jnp.bfloat16),
            pltpu.SemaphoreType.DMA((2,)),
            pltpu.SemaphoreType.DMA((STRIPS,)),
        ],
        compiler_params=pltpu.CompilerParams(vmem_limit_bytes=62 * 2**20),
        name="state",
    )(keys, values)


def read_state(scale, queries, state):
    tokens = queries.shape[0]
    return pl.pallas_call(
        read_kernel,
        out_shape=jax.ShapeDtypeStruct((tokens, WIDE), jnp.bfloat16),
        in_specs=[pl.BlockSpec(memory_space=pltpu.SMEM), in_vmem(), in_vmem()],
        out_specs=in_vmem(),
        scratch_shapes=[
            pltpu.VMEM((WIDE, tokens), jnp.float32),
            pltpu.VMEM((WIDE, tokens), jnp.bfloat16),
            pltpu.VMEM((HEADS, ROWS, tokens), jnp.bfloat16),
            pltpu.VMEM((HD, STRIPS * STRIP * WIDE), jnp.float32),
        ],
        compiler_params=pltpu.CompilerParams(vmem_limit_bytes=48 * 2**20),
        name="read",
    )(scale, queries, state)


def on_device(queries, keys, values):
    plane = lax.axis_size(PLANE)
    groups = lax.axis_size(("pair", "core"))
    shards = plane // groups
    layers = lax.axis_size(DEPTH)
    count = (lax.axis_index(DEPTH + ("pair", "core")) + 1).astype(jnp.float32)
    scale = (1.0 / (HD * jnp.sqrt(count * (queries.shape[0] * shards)))).reshape(1)
    order = np.arange(layers).reshape([lax.axis_size(axis) for axis in DEPTH]).T.reshape(-1)
    earlier = (jnp.asarray(order) < lax.axis_index(DEPTH)).astype(jnp.float32)
    local = make_state(keys, values)
    part = local.shape[1:]
    local, earlier, scale = lax.optimization_barrier((local, earlier, scale))
    arrived = lax.all_to_all(local, PLANE, 0, 0, tiled=True)
    totals = jnp.sum(arrived.reshape(groups, shards, *part).astype(jnp.float32), 1)
    whole = jnp.sum(totals, 0).astype(jnp.bfloat16)
    copies = jnp.broadcast_to(whole[None], (layers, *part))
    copies, totals, earlier, scale = lax.optimization_barrier((copies, totals, earlier, scale))
    others = lax.all_to_all(copies, DEPTH[::-1], 0, 0, tiled=True)
    before = jnp.sum(others.astype(jnp.float32) * earlier[:, None, None], 0)
    running = []
    for group in range(groups):
        before = before + totals[group]
        running.append(before.astype(jnp.bfloat16))
    inclusive = jnp.stack(running)
    copies = jnp.broadcast_to(inclusive[:, None], (groups, shards, *part))
    copies, scale = lax.optimization_barrier((copies.reshape(plane, *part), scale))
    state = lax.all_to_all(copies, PLANE, 0, 0, tiled=True)
    state, scale = lax.optimization_barrier((state, scale))
    return read_state(scale, queries, state)


def solution(mesh):
    torus = Mesh(mesh.devices.reshape(2, 2, 2, 2, 2, 2, 4), EVERY)
    spec = P(EVERY, None)
    return jax.shard_map(
        on_device, mesh=torus, in_specs=(spec, spec, spec), out_specs=spec, check_vma=False
    )
```

time: 66.4 us -> 64.4 us (0.970)
  blocking collectives: 54.6 us -> 52.9 us
  Pallas kernels: 10.9 us -> 10 us
    all_to_all x1, blocking collectives: 16.3 us -> 14.8 us  [on_device(): others = lax.all_to_all(copies, DEPTH[::-1], 0, 0, tiled=True)]
    pallas_call x1, Pallas kernels: 6.78 us -> 5.43 us  [make_state(): pl.pallas_call(state_kernel, out_shape=jax.ShapeDtypeStruct((PARTS, *part...]
where the time goes in v5:
time: 64.4 us; the launch traced here: 64.1 us
  blocking collectives  52.9 us (82%)
  Pallas kernels  10 us (16%)
  other arithmetic  0.98 us (2%)
    all_to_all x1, blocking collectives, on_device(): arrived = lax.all_to_all(local, PLANE, 0, 0, tiled=True)  20.6 us
    all_to_all x1, blocking collectives, on_device(): state = lax.all_to_all(copies, PLANE, 0, 0, tiled=True)  17.5 us
    all_to_all x1, blocking collectives, on_device(): others = lax.all_to_all(copies, DEPTH[::-1], 0, 0, tiled=True)  14.8 us
    pallas_call x1, Pallas kernels, make_state(): pl.pallas_call(state_kernel, out_shape=jax.ShapeDtypeStruct((PARTS, *part...  5.43 us
    pallas_call x1, Pallas kernels, read_state(): pl.pallas_call(read_kernel, out_shape=jax.ShapeDtypeStruct((tokens, WIDE)...  4.57 us

profile of v5, /device:TPU:1, one launch (start us, length us, event | category | flops | bytes accessed | tf_op | source)
XLA Modules:
  0.0 64.1 jit_solution(4988055716766167868)
XLA Ops:
  0.1 0.7 %compare_convert_fusion = f32[8]{0:T(128)S(1)} fusion(s32[8]{0:T(128)} %constant.44.clone, s32[]{:T(128)S(6)} %add.44), kind=kLoop, calls=%fused_computation.8 | loop fusion | flops 16 | bytes 68 | tf_op jit(solution)/shard_map/convert_element_type | solution.py:183
  0.8 5.4 %state.1 = bf16[32,8,1152]{2,1,0:T(8,128)(2,1)} custom-call(bf16[2048,128]{1,0:T(8,128)(2,1)} %keys_far.1, bf16[2048,128]{1,0:T(8,128)(2,1)} %values_far.1), custom_call_target="tpu_custom_call" | custom-call | tf_op jit(solution)/shard_map/state/pallas_call | solution.py:140
  6.2 20.6 %all_to_all.15 = bf16[32,8,1152]{2,1,0:T(8,128)(2,1)S(1)} all-to-all(bf16[32,8,1152]{2,1,0:T(8,128)(2,1)} %state.1), channel_id=1, replica_groups=mesh['depth_0'=2,'depth_1'=2,'depth_2'=2,'pair'=2,'core'=2,'near'=2,'row..., dimensions={0} | all-to-all | bytes 1179648 | tf_op jit(solution)/shard_map/all_to_all | solution.py:187
  26.8 0.1 convert_reduce_fusion
  26.9 0.1 reduce_sum.32
  27.0 14.8 %all_to_all.16 = bf16[8,8,1152]{2,1,0:T(8,128)(2,1)S(1)} all-to-all(bf16[8,8,1152]{2,1,0:T(8,128)(2,1)S(1)} %broadcast_in_dim.4), channel_id=1, replica_groups=mesh['depth_0'=2,'depth_1'=2,'depth_2'=2,'pair'=2,'core'=2,'near'=2,'row..., dimensions={0} | all-to-all | bytes 294912 | tf_op jit(solution)/shard_map/all_to_all | solution.py:192
  41.8 0.1 multiply_reduce_fusion
  42.0 0.0 copy-start
  42.0 17.5 %all_to_all.17.state = bf16[32,8,1152]{2,1,0:T(8,128)(2,1)S(1)} all-to-all(bf16[32,8,1152]{2,1,0:T(8,128)(2,1)S(1)} %bitcast.8), channel_id=1, replica_groups=mesh['depth_0'=2,'depth_1'=2,'depth_2'=2,'pair'=2,'core'=2,'near'=2,'row..., dimensions={0} | all-to-all | bytes 1179648 | tf_op jit(solution)/shard_map/all_to_all | solution.py:201
  59.5 0.0 copy-done
  59.5 4.6 %read.1 = bf16[2048,128]{1,0:T(8,128)(2,1)} custom-call(f32[1]{0:T(128)} %bitcast.scale, bf16[2048,128]{1,0:T(8,128)(2,1)S(1)} %copy-done, bf16[32,8,1152]{2,1,0:T(8,128)(2,1)S(1)} %all_to_all.17.state), custom_call_target="tpu_custom_call" | custom-call | tf_op jit(solution)/shard_map/read/pallas_call | solution.py:159
  (5 shorter events, 0.1 us)
Async XLA Ops:
  42.0 17.6 %copy-start = (bf16[2048,128]{1,0:T(8,128)(2,1)S(1)}, bf16[2048,128]{1,0:T(8,128)(2,1)}, u32[]{:S(2)}) copy-start(bf16[2048,128]{1,0:T(8,128)(2,1)} %queries.1) | copy-start | bytes 1572868

commit v6 on v5

v6 whole, which is shorter than its diff:
```python
import jax
import jax.numpy as jnp
from jax import lax
from jax.experimental import pallas as pl
from jax.experimental.pallas import tpu as pltpu
from jax.sharding import Mesh
from jax.sharding import PartitionSpec as P

HD = 64
HEADS = 2
WIDE = HEADS * HD
BLOCK = 16
BLOCKS = HD // BLOCK
TURNS = BLOCK // 2
BAND = 2 * HD
ROWS = 2 * TURNS * BAND + HD
STRIP = 9
TALL = 8
PARTS = 2 * WIDE // TALL

DEPTH = ("depth_0", "depth_1", "depth_2")
PLANE = ("pair", "core", "near", "row")
EVERY = DEPTH + PLANE


def across(wide, swap, move=0, turn=0):
    rows = []
    for head in (1, 0) if swap else (0, 1):
        mine = wide[HD * head : HD * head + HD]
        if move:
            mine = jnp.concatenate([mine[BLOCK * (move % BLOCKS) :], mine[: BLOCK * (move % BLOCKS)]], 0)
        if turn:
            mine = pltpu.roll(mine, HD - turn, 0)
        rows.append(mine)
    return jnp.concatenate(rows, 0).astype(jnp.bfloat16).T


def state_kernel(keys_far, values_far, out_far, keys, values, out, arrived, left):
    loads = [
        pltpu.make_async_copy(keys_far, keys, arrived.at[0]),
        pltpu.make_async_copy(values_far, values, arrived.at[1]),
    ]
    for load in loads:
        load.start()
    stores = []

    def store(strip, begin, end):
        parts = pl.ds(WIDE // TALL * strip, WIDE // TALL)
        lanes = pl.ds(BAND * begin, BAND * (end - begin))
        stores.append(
            pltpu.make_async_copy(out.at[parts, :, lanes], out_far.at[parts, :, lanes], left.at[len(stores)])
        )
        stores[-1].start()

    def put(place, heads):
        strip, place = divmod(place, STRIP)
        for k in range(WIDE // TALL):
            head, row = divmod(k * TALL, HD)
            part = heads[head][row : row + TALL].astype(out.dtype)
            out[WIDE // TALL * strip + k, :, pl.ds(BAND * place, BAND)] = part

    loads[0].wait()
    x = keys[...]
    wide = x.astype(jnp.float32).T
    first = [x, across(wide, False, -1)], [across(wide, True), across(wide, True, -1)]
    loads[1].wait()
    turned_values = values[...].astype(jnp.float32).T.astype(jnp.bfloat16)
    lane = lax.broadcasted_iota(jnp.int32, (1, BAND), 1)
    for s in range(TURNS):
        others = across(wide, False, 0, s) if s else x, across(wide, True, 0, s + TURNS)
        feats = jnp.concatenate([first[swap][k] * others[swap] for k in range(2) for swap in range(2)], 1)
        product = jnp.dot(turned_values, feats, preferred_element_type=jnp.float32)
        for k in range(2):
            plain, swapped = (product[:, BAND * j : BAND * j + BAND] for j in (2 * k, 2 * k + 1))
            heads = [
                jnp.where(lane < HD, plain[:HD], swapped[:HD]),
                jnp.where(lane < HD, swapped[HD:], plain[HD:]),
            ]
            for head in range(HEADS):
                once = (lane < HD) == (head == 0) if s == 0 and k == 0 else lane < 0
                heads[head] = heads[head] * jnp.where(once, 1.0, 2.0)
            put(2 * s + k, heads)
        if 2 * s + 2 == STRIP + 1:
            store(0, 0, STRIP)
        if s == TURNS - 2:
            store(1, 0, 2 * s + 2 - STRIP)
    feats = jnp.concatenate([first[swap][0] * across(wide, swap == 1, 2) for swap in range(2)], 1)
    product = jnp.dot(turned_values, feats, preferred_element_type=jnp.float32)
    heads = []
    for head in range(HEADS):
        mine = product[HD * head : HD * head + HD, BAND * head : BAND * head + BAND]
        heads.append(jnp.where(lane < HD, mine, 0.0))
    put(2 * TURNS, heads)
    put(2 * TURNS + 1, [jnp.zeros((HD, BAND), jnp.float32)] * HEADS)
    store(1, 2 * TURNS - 2 - STRIP, STRIP)
    for copy in stores:
        copy.wait()


def query_band(flat, plain, head, s):
    rows = pl.ds(head * HD, HD)
    x = plain[rows, :]
    blocks = [plain[pl.ds(head * HD + k * BLOCK, BLOCK), :] for k in range(BLOCKS)]
    if s == TURNS:
        return x * jnp.concatenate(blocks[2:] + blocks[:2], 0)
    lifted = jnp.concatenate(blocks[-1:] + blocks[:-1], 0)
    turns = (s, s + TURNS) if head == 0 else (s + TURNS, s)
    others = [pltpu.roll(flat[rows, :], HD - t, 0).astype(jnp.bfloat16) if t else x for t in turns]
    return jnp.concatenate([first * other for first in (x, lifted) for other in others], 0)


def read_kernel(scale, queries, state, out, flat, plain, feats, whole):
    for k in range(PARTS):
        strip, rows = divmod(k, WIDE // TALL)
        whole[pl.ds(TALL * rows, TALL), pl.ds(STRIP * BAND * strip, STRIP * BAND)] = state[k].astype(jnp.float32)
    wide = queries[...].astype(jnp.float32).T
    flat[...] = wide
    plain[...] = wide.astype(jnp.bfloat16)
    both = []
    for head in range(HEADS):
        product = jnp.zeros((HD, queries.shape[0]), jnp.float32)
        begin = 0
        for s in range(TURNS + 1):
            value = query_band(flat, plain, head, s)
            end = 2 * s * BAND + value.shape[0]
            feats[head, pl.ds(2 * s * BAND, value.shape[0]), :] = value
            if s != TURNS - 1:
                here = whole[pl.ds(head * HD, HD), :][:, begin:end].astype(jnp.bfloat16)
                right = feats[head, pl.ds(begin, end - begin), :]
                product += jnp.dot(here, right, preferred_element_type=jnp.float32)
                begin = end
        both.append(product)
    result = jnp.concatenate(both, 0) * scale[0]
    out[...] = result.T.astype(out.dtype)


def in_vmem():
    return pl.BlockSpec(memory_space=pltpu.VMEM)


def in_hbm():
    return pl.BlockSpec(memory_space=pltpu.HBM)


def make_state(keys, values):
    tokens = keys.shape[0]
    part = (TALL, STRIP * BAND)
    return pl.pallas_call(
        state_kernel,
        out_shape=jax.ShapeDtypeStruct((PARTS, *part), jnp.bfloat16),
        in_specs=[in_hbm(), in_hbm()],
        out_specs=in_hbm(),
        scratch_shapes=[
            pltpu.VMEM((tokens, WIDE), jnp.bfloat16),
            pltpu.VMEM((tokens, WIDE), jnp.bfloat16),
            pltpu.VMEM((PARTS, *part), jnp.bfloat16),
            pltpu.SemaphoreType.DMA((2,)),
            pltpu.SemaphoreType.DMA((3,)),
        ],
        compiler_params=pltpu.CompilerParams(vmem_limit_bytes=62 * 2**20),
        name="state",
    )(keys, values)


def read_state(scale, queries, state):
    tokens = queries.shape[0]
    return pl.pallas_call(
        read_kernel,
        out_shape=jax.ShapeDtypeStruct((tokens, WIDE), jnp.bfloat16),
        in_specs=[pl.BlockSpec(memory_space=pltpu.SMEM), in_vmem(), in_vmem()],
        out_specs=in_vmem(),
        scratch_shapes=[
            pltpu.VMEM((WIDE, tokens), jnp.float32),
            pltpu.VMEM((WIDE, tokens), jnp.bfloat16),
            pltpu.VMEM((HEADS, ROWS, tokens), jnp.bfloat16),
            pltpu.VMEM((WIDE, 2 * STRIP * BAND), jnp.float32),
        ],
        compiler_params=pltpu.CompilerParams(vmem_limit_bytes=48 * 2**20),
        name="read",
    )(scale, queries, state)


def on_device(queries, keys, values):
    plane = lax.axis_size(PLANE)
    groups = lax.axis_size(("pair", "core"))
    shards = plane // groups
    layers = lax.axis_size(DEPTH)
    count = (lax.axis_index(DEPTH + ("pair", "core")) + 1).astype(jnp.float32)
    scale = (1.0 / (HD * jnp.sqrt(count * (queries.shape[0] * shards)))).reshape(1)
    order, place = 0, lax.iota(jnp.int32, layers)
    for axis in DEPTH:
        size = lax.axis_size(axis)
        order, place = order * size + place % size, place // size
    earlier = (order < lax.axis_index(DEPTH)).astype(jnp.float32)
    local = make_state(keys, values)
    part = local.shape[1:]
    local, earlier, scale = lax.optimization_barrier((local, earlier, scale))
    arrived = lax.all_to_all(local, PLANE, 0, 0, tiled=True)
    totals = jnp.sum(arrived.reshape(groups, shards, *part).astype(jnp.float32), 1)
    whole = jnp.sum(totals, 0).astype(jnp.bfloat16)
    copies = jnp.broadcast_to(whole[None], (layers, *part))
    copies, totals, earlier, scale = lax.optimization_barrier((copies, totals, earlier, scale))
    others = lax.all_to_all(copies, DEPTH[::-1], 0, 0, tiled=True)
    before = jnp.sum(others.astype(jnp.float32) * earlier[:, None, None], 0)
    running = []
    for group in range(groups):
        before = before + totals[group]
        running.append(before.astype(jnp.bfloat16))
    inclusive = jnp.stack(running)
    copies = jnp.broadcast_to(inclusive[:, None], (groups, shards, *part))
    copies, scale = lax.optimization_barrier((copies.reshape(plane, *part), scale))
    state = lax.all_to_all(copies, PLANE, 0, 0, tiled=True)
    state, scale = lax.optimization_barrier((state, scale))
    return read_state(scale, queries, state)


def solution(mesh):
    torus = Mesh(mesh.devices.reshape(2, 2, 2, 2, 2, 2, 4), EVERY)
    spec = P(EVERY, None)
    return jax.shard_map(
        on_device, mesh=torus, in_specs=(spec, spec, spec), out_specs=spec, check_vma=False
    )
```

time: 64.4 us -> 63.5 us (0.986)
  other arithmetic: 0.98 us -> 0.33 us
    convert_element_type x1, other arithmetic: 0.66 us -> 0.02 us  [on_device(): earlier = (order < lax.axis_index(DEPTH)).astype(jnp.float32)]
where the time goes in v6:
time: 63.5 us; the launch traced here: 63.3 us
  blocking collectives  52.9 us (83%)
  Pallas kernels  9.81 us (15%)
    all_to_all x1, blocking collectives, on_device(): arrived = lax.all_to_all(local, PLANE, 0, 0, tiled=True)  20.6 us
    all_to_all x1, blocking collectives, on_device(): state = lax.all_to_all(copies, PLANE, 0, 0, tiled=True)  17.5 us
    all_to_all x1, blocking collectives, on_device(): others = lax.all_to_all(copies, DEPTH[::-1], 0, 0, tiled=True)  14.8 us
    pallas_call x1, Pallas kernels, make_state(): pl.pallas_call(state_kernel, out_shape=jax.ShapeDtypeStruct((PARTS, *part...  5.5 us
    pallas_call x1, Pallas kernels, read_state(): pl.pallas_call(read_kernel, out_shape=jax.ShapeDtypeStruct((tokens, WIDE)...  4.31 us

profile of v6, /device:TPU:1, one launch (start us, length us, event | category | flops | bytes accessed | tf_op | source)
XLA Modules:
  0.0 63.3 jit_solution(9468797520997568459)
XLA Ops:
  0.1 5.5 %state.1 = bf16[32,8,1152]{2,1,0:T(8,128)(2,1)} custom-call(bf16[2048,128]{1,0:T(8,128)(2,1)} %keys_far.1, bf16[2048,128]{1,0:T(8,128)(2,1)} %values_far.1), custom_call_target="tpu_custom_call" | custom-call | tf_op jit(solution)/shard_map/state/pallas_call | solution.py:148
  5.6 20.6 %all_to_all.15 = bf16[32,8,1152]{2,1,0:T(8,128)(2,1)S(1)} all-to-all(bf16[32,8,1152]{2,1,0:T(8,128)(2,1)} %state.1), channel_id=1, replica_groups=mesh['depth_0'=2,'depth_1'=2,'depth_2'=2,'pair'=2,'core'=2,'near'=2,'row..., dimensions={0} | all-to-all | bytes 1179648 | tf_op jit(solution)/shard_map/all_to_all | solution.py:198
  26.2 0.1 convert_reduce_fusion
  26.3 0.1 reduce_sum.32
  26.4 14.8 %all_to_all.16 = bf16[8,8,1152]{2,1,0:T(8,128)(2,1)S(1)} all-to-all(bf16[8,8,1152]{2,1,0:T(8,128)(2,1)S(1)} %broadcast_in_dim.4), channel_id=1, replica_groups=mesh['depth_0'=2,'depth_1'=2,'depth_2'=2,'pair'=2,'core'=2,'near'=2,'row..., dimensions={0} | all-to-all | bytes 294912 | tf_op jit(solution)/shard_map/all_to_all | solution.py:203
  41.2 0.1 multiply_reduce_fusion
  41.4 0.0 copy-start
  41.4 17.5 %all_to_all.17.state = bf16[32,8,1152]{2,1,0:T(8,128)(2,1)S(1)} all-to-all(bf16[32,8,1152]{2,1,0:T(8,128)(2,1)S(1)} %bitcast.8), channel_id=1, replica_groups=mesh['depth_0'=2,'depth_1'=2,'depth_2'=2,'pair'=2,'core'=2,'near'=2,'row..., dimensions={0} | all-to-all | bytes 1179648 | tf_op jit(solution)/shard_map/all_to_all | solution.py:212
  59.0 0.0 copy-done
  59.0 4.3 %read.1 = bf16[2048,128]{1,0:T(8,128)(2,1)} custom-call(f32[1]{0:T(128)} %bitcast.scale, bf16[2048,128]{1,0:T(8,128)(2,1)S(1)} %copy-done, bf16[32,8,1152]{2,1,0:T(8,128)(2,1)S(1)} %all_to_all.17.state), custom_call_target="tpu_custom_call" | custom-call | tf_op jit(solution)/shard_map/read/pallas_call | solution.py:167
  (6 shorter events, 0.1 us)
Async XLA Ops:
  41.4 17.6 %copy-start = (bf16[2048,128]{1,0:T(8,128)(2,1)S(1)}, bf16[2048,128]{1,0:T(8,128)(2,1)}, u32[]{:S(2)}) copy-start(bf16[2048,128]{1,0:T(8,128)(2,1)} %queries.1) | copy-start | bytes 1572868

commit v7 on v6

--- a/solution.py
+++ b/solution.py
@@ -16,6 +16,7 @@
 ROWS = 2 * TURNS * BAND + HD
 STRIP = 9
 TALL = 8
+READS = 2
 PARTS = 2 * WIDE // TALL
 
 DEPTH = ("depth_0", "depth_1", "depth_2")
@@ -97,41 +98,52 @@
         copy.wait()
 
 
-def query_band(flat, plain, head, s):
+def query_band(flat, plain, head, s, lanes):
     rows = pl.ds(head * HD, HD)
-    x = plain[rows, :]
-    blocks = [plain[pl.ds(head * HD + k * BLOCK, BLOCK), :] for k in range(BLOCKS)]
+    x = plain[rows, lanes]
+    blocks = [plain[pl.ds(head * HD + k * BLOCK, BLOCK), lanes] for k in range(BLOCKS)]
     if s == TURNS:
         return x * jnp.concatenate(blocks[2:] + blocks[:2], 0)
     lifted = jnp.concatenate(blocks[-1:] + blocks[:-1], 0)
     turns = (s, s + TURNS) if head == 0 else (s + TURNS, s)
-    others = [pltpu.roll(flat[rows, :], HD - t, 0).astype(jnp.bfloat16) if t else x for t in turns]
+    others = [pltpu.roll(flat[rows, lanes], HD - t, 0).astype(jnp.bfloat16) if t else x for t in turns]
     return jnp.concatenate([first * other for first in (x, lifted) for other in others], 0)
 
 
-def read_kernel(scale, queries, state, out, flat, plain, feats, whole):
+def read_kernel(scale, queries, state, out_far, out, flat, plain, feats, whole, sent):
     for k in range(PARTS):
         strip, rows = divmod(k, WIDE // TALL)
         whole[pl.ds(TALL * rows, TALL), pl.ds(STRIP * BAND * strip, STRIP * BAND)] = state[k].astype(jnp.float32)
     wide = queries[...].astype(jnp.float32).T
     flat[...] = wide
     plain[...] = wide.astype(jnp.bfloat16)
-    both = []
+    tokens = queries.shape[0]
+    products, stores = [], []
     for head in range(HEADS):
-        product = jnp.zeros((HD, queries.shape[0]), jnp.float32)
-        begin = 0
-        for s in range(TURNS + 1):
-            value = query_band(flat, plain, head, s)
-            end = 2 * s * BAND + value.shape[0]
-            feats[head, pl.ds(2 * s * BAND, value.shape[0]), :] = value
-            if s != TURNS - 1:
-                here = whole[pl.ds(head * HD, HD), :][:, begin:end].astype(jnp.bfloat16)
-                right = feats[head, pl.ds(begin, end - begin), :]
-                product += jnp.dot(here, right, preferred_element_type=jnp.float32)
-                begin = end
-        both.append(product)
-    result = jnp.concatenate(both, 0) * scale[0]
-    out[...] = result.T.astype(out.dtype)
+        count = 1 if head == 0 else READS
+        size = tokens // count
+        for k in range(count):
+            lanes = pl.ds(k * size, size)
+            product = jnp.zeros((HD, size), jnp.float32)
+            begin = 0
+            for s in range(TURNS + 1):
+                value = query_band(flat, plain, head, s, lanes)
+                end = 2 * s * BAND + value.shape[0]
+                feats[head, pl.ds(2 * s * BAND, value.shape[0]), lanes] = value
+                if s != TURNS - 1:
+                    here = whole[pl.ds(head * HD, HD), :][:, begin:end].astype(jnp.bfloat16)
+                    right = feats[head, pl.ds(begin, end - begin), lanes]
+                    product += jnp.dot(here, right, preferred_element_type=jnp.float32)
+                    begin = end
+            if head == 0:
+                products.append(product)
+                continue
+            both = jnp.concatenate([products[0][:, k * size : k * size + size], product], 0) * scale[0]
+            out[lanes, :] = both.T.astype(out.dtype)
+            stores.append(pltpu.make_async_copy(out.at[lanes], out_far.at[lanes], sent.at[k]))
+            stores[-1].start()
+    for store in stores:
+        store.wait()
 
 
 def in_vmem():
@@ -168,12 +180,14 @@
         read_kernel,
         out_shape=jax.ShapeDtypeStruct((tokens, WIDE), jnp.bfloat16),
         in_specs=[pl.BlockSpec(memory_space=pltpu.SMEM), in_vmem(), in_vmem()],
-        out_specs=in_vmem(),
+        out_specs=in_hbm(),
         scratch_shapes=[
+            pltpu.VMEM((tokens, WIDE), jnp.bfloat16),
             pltpu.VMEM((WIDE, tokens), jnp.float32),
             pltpu.VMEM((WIDE, tokens), jnp.bfloat16),
             pltpu.VMEM((HEADS, ROWS, tokens), jnp.bfloat16),
             pltpu.VMEM((WIDE, 2 * STRIP * BAND), jnp.float32),
+            pltpu.SemaphoreType.DMA((READS,)),
         ],
         compiler_params=pltpu.CompilerParams(vmem_limit_bytes=48 * 2**20),
         name="read",

time: 63.5 us -> 63.5 us (level)
  no operation moved by 1% of the time
where the time goes in v7:
time: 63.5 us; the launch traced here: 63.2 us
  blocking collectives  52.9 us (83%)
  Pallas kernels  9.74 us (15%)
    all_to_all x1, blocking collectives, on_device(): arrived = lax.all_to_all(local, PLANE, 0, 0, tiled=True)  20.6 us
    all_to_all x1, blocking collectives, on_device(): state = lax.all_to_all(copies, PLANE, 0, 0, tiled=True)  17.5 us
    all_to_all x1, blocking collectives, on_device(): others = lax.all_to_all(copies, DEPTH[::-1], 0, 0, tiled=True)  14.8 us
    pallas_call x1, Pallas kernels, make_state(): pl.pallas_call(state_kernel, out_shape=jax.ShapeDtypeStruct((PARTS, *part...  5.5 us
    pallas_call x1, Pallas kernels, read_state(): pl.pallas_call(read_kernel, out_shape=jax.ShapeDtypeStruct((tokens, WIDE)...  4.24 us

profile of v7, /device:TPU:1, one launch (start us, length us, event | category | flops | bytes accessed | tf_op | source)
XLA Modules:
  0.0 63.2 jit_solution(6762002707401997311)
XLA Ops:
  0.1 5.5 %state.1 = bf16[32,8,1152]{2,1,0:T(8,128)(2,1)} custom-call(bf16[2048,128]{1,0:T(8,128)(2,1)} %keys_far.1, bf16[2048,128]{1,0:T(8,128)(2,1)} %values_far.1), custom_call_target="tpu_custom_call" | custom-call | tf_op jit(solution)/shard_map/state/pallas_call | solution.py:160
  5.6 20.6 %all_to_all.15 = bf16[32,8,1152]{2,1,0:T(8,128)(2,1)S(1)} all-to-all(bf16[32,8,1152]{2,1,0:T(8,128)(2,1)} %state.1), channel_id=1, replica_groups=mesh['depth_0'=2,'depth_1'=2,'depth_2'=2,'pair'=2,'core'=2,'near'=2,'row..., dimensions={0} | all-to-all | bytes 1179648 | tf_op jit(solution)/shard_map/all_to_all | solution.py:212
  26.2 0.1 convert_reduce_fusion
  26.3 0.1 reduce_sum.32
  26.4 14.8 %all_to_all.16 = bf16[8,8,1152]{2,1,0:T(8,128)(2,1)S(1)} all-to-all(bf16[8,8,1152]{2,1,0:T(8,128)(2,1)S(1)} %broadcast_in_dim.4), channel_id=1, replica_groups=mesh['depth_0'=2,'depth_1'=2,'depth_2'=2,'pair'=2,'core'=2,'near'=2,'row..., dimensions={0} | all-to-all | bytes 294912 | tf_op jit(solution)/shard_map/all_to_all | solution.py:217
  41.2 0.1 multiply_reduce_fusion
  41.4 0.0 copy-start
  41.4 17.5 %all_to_all.17.state = bf16[32,8,1152]{2,1,0:T(8,128)(2,1)S(1)} all-to-all(bf16[32,8,1152]{2,1,0:T(8,128)(2,1)S(1)} %bitcast.8), channel_id=1, replica_groups=mesh['depth_0'=2,'depth_1'=2,'depth_2'=2,'pair'=2,'core'=2,'near'=2,'row..., dimensions={0} | all-to-all | bytes 1179648 | tf_op jit(solution)/shard_map/all_to_all | solution.py:226
  59.0 0.0 copy-done
  59.0 4.2 %read.1 = bf16[2048,128]{1,0:T(8,128)(2,1)} custom-call(f32[1]{0:T(128)} %bitcast.scale, bf16[2048,128]{1,0:T(8,128)(2,1)S(1)} %copy-done, bf16[32,8,1152]{2,1,0:T(8,128)(2,1)S(1)} %all_to_all.17.state), custom_call_target="tpu_custom_call" | custom-call | tf_op jit(solution)/shard_map/read/pallas_call | solution.py:179
  (6 shorter events, 0.1 us)
Async XLA Ops:
  41.4 17.6 %copy-start = (bf16[2048,128]{1,0:T(8,128)(2,1)S(1)}, bf16[2048,128]{1,0:T(8,128)(2,1)}, u32[]{:S(2)}) copy-start(bf16[2048,128]{1,0:T(8,128)(2,1)} %queries.1) | copy-start | bytes 1572868

commit v8 on v7

--- a/solution.py
+++ b/solution.py
@@ -110,7 +110,7 @@
     return jnp.concatenate([first * other for first in (x, lifted) for other in others], 0)
 
 
-def read_kernel(scale, queries, state, out_far, out, flat, plain, feats, whole, sent):
+def read_kernel(queries, state, out_far, out, flat, plain, feats, whole, sent):
     for k in range(PARTS):
         strip, rows = divmod(k, WIDE // TALL)
         whole[pl.ds(TALL * rows, TALL), pl.ds(STRIP * BAND * strip, STRIP * BAND)] = state[k].astype(jnp.float32)
@@ -138,7 +138,7 @@
             if head == 0:
                 products.append(product)
                 continue
-            both = jnp.concatenate([products[0][:, k * size : k * size + size], product], 0) * scale[0]
+            both = jnp.concatenate([products[0][:, k * size : k * size + size], product], 0)
             out[lanes, :] = both.T.astype(out.dtype)
             stores.append(pltpu.make_async_copy(out.at[lanes], out_far.at[lanes], sent.at[k]))
             stores[-1].start()
@@ -174,12 +174,12 @@
     )(keys, values)
 
 
-def read_state(scale, queries, state):
+def read_state(queries, state):
     tokens = queries.shape[0]
     return pl.pallas_call(
         read_kernel,
         out_shape=jax.ShapeDtypeStruct((tokens, WIDE), jnp.bfloat16),
-        in_specs=[pl.BlockSpec(memory_space=pltpu.SMEM), in_vmem(), in_vmem()],
+        in_specs=[in_vmem(), in_vmem()],
         out_specs=in_hbm(),
         scratch_shapes=[
             pltpu.VMEM((tokens, WIDE), jnp.bfloat16),
@@ -191,7 +191,7 @@
         ],
         compiler_params=pltpu.CompilerParams(vmem_limit_bytes=48 * 2**20),
         name="read",
-    )(scale, queries, state)
+    )(queries, state)
 
 
 def on_device(queries, keys, values):
@@ -199,8 +199,9 @@
     groups = lax.axis_size(("pair", "core"))
     shards = plane // groups
     layers = lax.axis_size(DEPTH)
-    count = (lax.axis_index(DEPTH + ("pair", "core")) + 1).astype(jnp.float32)
-    scale = (1.0 / (HD * jnp.sqrt(count * (queries.shape[0] * shards)))).reshape(1)
+    first = lax.axis_index(DEPTH) * groups + 1
+    tokens = queries.shape[0] * shards
+    scale = [1.0 / (HD * jnp.sqrt((first + k).astype(jnp.float32) * tokens)) for k in range(groups)]
     order, place = 0, lax.iota(jnp.int32, layers)
     for axis in DEPTH:
         size = lax.axis_size(axis)
@@ -219,13 +220,11 @@
     running = []
     for group in range(groups):
         before = before + totals[group]
-        running.append(before.astype(jnp.bfloat16))
+        running.append((before * scale[group]).astype(jnp.bfloat16))
     inclusive = jnp.stack(running)
     copies = jnp.broadcast_to(inclusive[:, None], (groups, shards, *part))
-    copies, scale = lax.optimization_barrier((copies.reshape(plane, *part), scale))
-    state = lax.all_to_all(copies, PLANE, 0, 0, tiled=True)
-    state, scale = lax.optimization_barrier((state, scale))
-    return read_state(scale, queries, state)
+    state = lax.all_to_all(copies.reshape(plane, *part), PLANE, 0, 0, tiled=True)
+    return read_state(queries, state)
 
 
 def solution(mesh):

time: 63.5 us -> 63.7 us (level)
  no operation moved by 1% of the time
where the time goes in v8:
time: 63.7 us; the launch traced here: 63.4 us
  blocking collectives  52.9 us (83%)
  Pallas kernels  9.7 us (15%)
    all_to_all x1, blocking collectives, on_device(): arrived = lax.all_to_all(local, PLANE, 0, 0, tiled=True)  20.6 us
    all_to_all x1, blocking collectives, on_device(): lax.all_to_all(copies.reshape(plane, *part), PLANE, 0, 0, tiled=True)  17.5 us
    all_to_all x1, blocking collectives, on_device(): others = lax.all_to_all(copies, DEPTH[::-1], 0, 0, tiled=True)  14.8 us
    pallas_call x1, Pallas kernels, make_state(): pl.pallas_call(state_kernel, out_shape=jax.ShapeDtypeStruct((PARTS, *part...  5.5 us
    pallas_call x1, Pallas kernels, read_state(): pl.pallas_call(read_kernel, out_shape=jax.ShapeDtypeStruct((tokens, WIDE)...  4.2 us

profile of v8, /device:TPU:1, one launch (start us, length us, event | category | flops | bytes accessed | tf_op | source)
XLA Modules:
  0.0 63.4 jit_solution(15473731318031597913)
XLA Ops:
  0.4 5.5 %state.1 = bf16[32,8,1152]{2,1,0:T(8,128)(2,1)} custom-call(bf16[2048,128]{1,0:T(8,128)(2,1)} %keys_far.1, bf16[2048,128]{1,0:T(8,128)(2,1)} %values_far.1), custom_call_target="tpu_custom_call" | custom-call | tf_op jit(solution)/shard_map/state/pallas_call | solution.py:160
  5.9 20.6 %all_to_all.15 = bf16[32,8,1152]{2,1,0:T(8,128)(2,1)S(1)} all-to-all(bf16[32,8,1152]{2,1,0:T(8,128)(2,1)} %state.1), channel_id=1, replica_groups=mesh['depth_0'=2,'depth_1'=2,'depth_2'=2,'pair'=2,'core'=2,'near'=2,'row..., dimensions={0} | all-to-all | bytes 1179648 | tf_op jit(solution)/shard_map/all_to_all | solution.py:213
  26.5 0.1 convert_reduce_fusion
  26.5 0.1 reduce_sum.32
  26.7 14.8 %all_to_all.16 = bf16[8,8,1152]{2,1,0:T(8,128)(2,1)S(1)} all-to-all(bf16[8,8,1152]{2,1,0:T(8,128)(2,1)S(1)} %broadcast_in_dim.4), channel_id=1, replica_groups=mesh['depth_0'=2,'depth_1'=2,'depth_2'=2,'pair'=2,'core'=2,'near'=2,'row..., dimensions={0} | all-to-all | bytes 294912 | tf_op jit(solution)/shard_map/all_to_all | solution.py:218
  41.4 0.1 multiply_reduce_fusion
  41.7 0.0 copy-start
  41.7 17.5 %all_to_all.17.state = bf16[32,8,1152]{2,1,0:T(8,128)(2,1)S(1)} all-to-all(bf16[32,8,1152]{2,1,0:T(8,128)(2,1)S(1)} %bitcast.7), channel_id=1, replica_groups=mesh['depth_0'=2,'depth_1'=2,'depth_2'=2,'pair'=2,'core'=2,'near'=2,'row..., dimensions={0} | all-to-all | bytes 1179648 | tf_op jit(solution)/shard_map/all_to_all | solution.py:226
  59.2 0.0 copy-done
  59.2 4.2 %read.1 = bf16[2048,128]{1,0:T(8,128)(2,1)} custom-call(bf16[2048,128]{1,0:T(8,128)(2,1)S(1)} %copy-done, bf16[32,8,1152]{2,1,0:T(8,128)(2,1)S(1)} %all_to_all.17.state), custom_call_target="tpu_custom_call" | custom-call | tf_op jit(solution)/shard_map/read/pallas_call | solution.py:179
  (6 shorter events, 0.1 us)
Async XLA Ops:
  41.7 17.6 %copy-start = (bf16[2048,128]{1,0:T(8,128)(2,1)S(1)}, bf16[2048,128]{1,0:T(8,128)(2,1)}, u32[]{:S(2)}) copy-start(bf16[2048,128]{1,0:T(8,128)(2,1)} %queries.1) | copy-start | bytes 1572868

commit v9 on v7

--- a/solution.py
+++ b/solution.py
@@ -38,8 +38,8 @@
 
 def state_kernel(keys_far, values_far, out_far, keys, values, out, arrived, left):
     loads = [
-        pltpu.make_async_copy(keys_far, keys, arrived.at[0]),
-        pltpu.make_async_copy(values_far, values, arrived.at[1]),
+        pltpu.make_async_copy(values_far, values, arrived.at[0]),
+        pltpu.make_async_copy(keys_far, keys, arrived.at[1]),
     ]
     for load in loads:
         load.start()
@@ -61,12 +61,24 @@
             out[WIDE // TALL * strip + k, :, pl.ds(BAND * place, BAND)] = part
 
     loads[0].wait()
+    turned_values = values[...].astype(jnp.float32).T.astype(jnp.bfloat16)
+    loads[1].wait()
     x = keys[...]
     wide = x.astype(jnp.float32).T
     first = [x, across(wide, False, -1)], [across(wide, True), across(wide, True, -1)]
-    loads[1].wait()
-    turned_values = values[...].astype(jnp.float32).T.astype(jnp.bfloat16)
     lane = lax.broadcasted_iota(jnp.int32, (1, BAND), 1)
+    def half_band():
+        feats = jnp.concatenate([first[swap][0] * across(wide, swap == 1, 2) for swap in range(2)], 1)
+        product = jnp.dot(turned_values, feats, preferred_element_type=jnp.float32)
+        heads = []
+        for head in range(HEADS):
+            mine = product[HD * head : HD * head + HD, BAND * head : BAND * head + BAND]
+            heads.append(jnp.where(lane < HD, mine, 0.0))
+        put(2 * TURNS, heads)
+
+    put(2 * TURNS + 1, [jnp.zeros((HD, BAND), jnp.float32)] * HEADS)
+    half_band()
+    store(1, 2 * TURNS - STRIP, STRIP)
     for s in range(TURNS):
         others = across(wide, False, 0, s) if s else x, across(wide, True, 0, s + TURNS)
         feats = jnp.concatenate([first[swap][k] * others[swap] for k in range(2) for swap in range(2)], 1)
@@ -85,15 +97,7 @@
             store(0, 0, STRIP)
         if s == TURNS - 2:
             store(1, 0, 2 * s + 2 - STRIP)
-    feats = jnp.concatenate([first[swap][0] * across(wide, swap == 1, 2) for swap in range(2)], 1)
-    product = jnp.dot(turned_values, feats, preferred_element_type=jnp.float32)
-    heads = []
-    for head in range(HEADS):
-        mine = product[HD * head : HD * head + HD, BAND * head : BAND * head + BAND]
-        heads.append(jnp.where(lane < HD, mine, 0.0))
-    put(2 * TURNS, heads)
-    put(2 * TURNS + 1, [jnp.zeros((HD, BAND), jnp.float32)] * HEADS)
-    store(1, 2 * TURNS - 2 - STRIP, STRIP)
+    store(1, 2 * TURNS - 2 - STRIP, 2 * TURNS - STRIP)
     for copy in stores:
         copy.wait()
 
@@ -167,7 +171,7 @@
             pltpu.VMEM((tokens, WIDE), jnp.bfloat16),
             pltpu.VMEM((PARTS, *part), jnp.bfloat16),
             pltpu.SemaphoreType.DMA((2,)),
-            pltpu.SemaphoreType.DMA((3,)),
+            pltpu.SemaphoreType.DMA((4,)),
         ],
         compiler_params=pltpu.CompilerParams(vmem_limit_bytes=62 * 2**20),
         name="state",

time: 63.5 us -> 63.3 us (level)
  no operation moved by 1% of the time
where the time goes in v9:
time: 63.3 us; the launch traced here: 63 us
  blocking collectives  52.9 us (84%)
  Pallas kernels  9.55 us (15%)
    all_to_all x1, blocking collectives, on_device(): arrived = lax.all_to_all(local, PLANE, 0, 0, tiled=True)  20.6 us
    all_to_all x1, blocking collectives, on_device(): state = lax.all_to_all(copies, PLANE, 0, 0, tiled=True)  17.5 us
    all_to_all x1, blocking collectives, on_device(): others = lax.all_to_all(copies, DEPTH[::-1], 0, 0, tiled=True)  14.8 us
    pallas_call x1, Pallas kernels, make_state(): pl.pallas_call(state_kernel, out_shape=jax.ShapeDtypeStruct((PARTS, *part...  5.31 us
    pallas_call x1, Pallas kernels, read_state(): pl.pallas_call(read_kernel, out_shape=jax.ShapeDtypeStruct((tokens, WIDE)...  4.24 us

profile of v9, /device:TPU:1, one launch (start us, length us, event | category | flops | bytes accessed | tf_op | source)
XLA Modules:
  0.0 63.0 jit_solution(6036075371363717881)
XLA Ops:
  0.1 5.3 %state.1 = bf16[32,8,1152]{2,1,0:T(8,128)(2,1)} custom-call(bf16[2048,128]{1,0:T(8,128)(2,1)} %keys_far.1, bf16[2048,128]{1,0:T(8,128)(2,1)} %values_far.1), custom_call_target="tpu_custom_call" | custom-call | tf_op jit(solution)/shard_map/state/pallas_call | solution.py:164
  5.4 20.6 %all_to_all.15 = bf16[32,8,1152]{2,1,0:T(8,128)(2,1)S(1)} all-to-all(bf16[32,8,1152]{2,1,0:T(8,128)(2,1)} %state.1), channel_id=1, replica_groups=mesh['depth_0'=2,'depth_1'=2,'depth_2'=2,'pair'=2,'core'=2,'near'=2,'row..., dimensions={0} | all-to-all | bytes 1179648 | tf_op jit(solution)/shard_map/all_to_all | solution.py:216
  26.0 0.1 convert_reduce_fusion
  26.1 0.1 reduce_sum.32
  26.2 14.8 %all_to_all.16 = bf16[8,8,1152]{2,1,0:T(8,128)(2,1)S(1)} all-to-all(bf16[8,8,1152]{2,1,0:T(8,128)(2,1)S(1)} %broadcast_in_dim.4), channel_id=1, replica_groups=mesh['depth_0'=2,'depth_1'=2,'depth_2'=2,'pair'=2,'core'=2,'near'=2,'row..., dimensions={0} | all-to-all | bytes 294912 | tf_op jit(solution)/shard_map/all_to_all | solution.py:221
  41.0 0.1 multiply_reduce_fusion
  41.2 0.0 copy-start
  41.2 17.5 %all_to_all.17.state = bf16[32,8,1152]{2,1,0:T(8,128)(2,1)S(1)} all-to-all(bf16[32,8,1152]{2,1,0:T(8,128)(2,1)S(1)} %bitcast.8), channel_id=1, replica_groups=mesh['depth_0'=2,'depth_1'=2,'depth_2'=2,'pair'=2,'core'=2,'near'=2,'row..., dimensions={0} | all-to-all | bytes 1179648 | tf_op jit(solution)/shard_map/all_to_all | solution.py:230
  58.8 0.0 copy-done
  58.8 4.2 %read.1 = bf16[2048,128]{1,0:T(8,128)(2,1)} custom-call(f32[1]{0:T(128)} %bitcast.scale, bf16[2048,128]{1,0:T(8,128)(2,1)S(1)} %copy-done, bf16[32,8,1152]{2,1,0:T(8,128)(2,1)S(1)} %all_to_all.17.state), custom_call_target="tpu_custom_call" | custom-call | tf_op jit(solution)/shard_map/read/pallas_call | solution.py:183
  (6 shorter events, 0.1 us)
Async XLA Ops:
  41.2 17.6 %copy-start = (bf16[2048,128]{1,0:T(8,128)(2,1)S(1)}, bf16[2048,128]{1,0:T(8,128)(2,1)}, u32[]{:S(2)}) copy-start(bf16[2048,128]{1,0:T(8,128)(2,1)} %queries.1) | copy-start | bytes 1572868

commit v10 on v6

--- a/solution.py
+++ b/solution.py
@@ -37,8 +37,8 @@
 
 def state_kernel(keys_far, values_far, out_far, keys, values, out, arrived, left):
     loads = [
-        pltpu.make_async_copy(keys_far, keys, arrived.at[0]),
-        pltpu.make_async_copy(values_far, values, arrived.at[1]),
+        pltpu.make_async_copy(values_far, values, arrived.at[0]),
+        pltpu.make_async_copy(keys_far, keys, arrived.at[1]),
     ]
     for load in loads:
         load.start()
@@ -60,12 +60,25 @@
             out[WIDE // TALL * strip + k, :, pl.ds(BAND * place, BAND)] = part
 
     loads[0].wait()
+    turned_values = values[...].astype(jnp.float32).T.astype(jnp.bfloat16)
+    loads[1].wait()
     x = keys[...]
     wide = x.astype(jnp.float32).T
     first = [x, across(wide, False, -1)], [across(wide, True), across(wide, True, -1)]
-    loads[1].wait()
-    turned_values = values[...].astype(jnp.float32).T.astype(jnp.bfloat16)
     lane = lax.broadcasted_iota(jnp.int32, (1, BAND), 1)
+
+    def half_band():
+        feats = jnp.concatenate([first[swap][0] * across(wide, swap == 1, 2) for swap in range(2)], 1)
+        product = jnp.dot(turned_values, feats, preferred_element_type=jnp.float32)
+        heads = []
+        for head in range(HEADS):
+            mine = product[HD * head : HD * head + HD, BAND * head : BAND * head + BAND]
+            heads.append(jnp.where(lane < HD, mine, 0.0))
+        put(2 * TURNS, heads)
+
+    put(2 * TURNS + 1, [jnp.zeros((HD, BAND), jnp.float32)] * HEADS)
+    half_band()
+    store(1, 2 * TURNS - STRIP, STRIP)
     for s in range(TURNS):
         others = across(wide, False, 0, s) if s else x, across(wide, True, 0, s + TURNS)
         feats = jnp.concatenate([first[swap][k] * others[swap] for k in range(2) for swap in range(2)], 1)
@@ -84,15 +97,7 @@
             store(0, 0, STRIP)
         if s == TURNS - 2:
             store(1, 0, 2 * s + 2 - STRIP)
-    feats = jnp.concatenate([first[swap][0] * across(wide, swap == 1, 2) for swap in range(2)], 1)
-    product = jnp.dot(turned_values, feats, preferred_element_type=jnp.float32)
-    heads = []
-    for head in range(HEADS):
-        mine = product[HD * head : HD * head + HD, BAND * head : BAND * head + BAND]
-        heads.append(jnp.where(lane < HD, mine, 0.0))
-    put(2 * TURNS, heads)
-    put(2 * TURNS + 1, [jnp.zeros((HD, BAND), jnp.float32)] * HEADS)
-    store(1, 2 * TURNS - 2 - STRIP, STRIP)
+    store(1, 2 * TURNS - 2 - STRIP, 2 * TURNS - STRIP)
     for copy in stores:
         copy.wait()
 
@@ -109,29 +114,37 @@
     return jnp.concatenate([first * other for first in (x, lifted) for other in others], 0)
 
 
-def read_kernel(scale, queries, state, out, flat, plain, feats, whole):
-    for k in range(PARTS):
-        strip, rows = divmod(k, WIDE // TALL)
-        whole[pl.ds(TALL * rows, TALL), pl.ds(STRIP * BAND * strip, STRIP * BAND)] = state[k].astype(jnp.float32)
+def read_kernel(scale, queries, state, out_far, out, flat, plain, feats, sent):
+    def rows_of(head):
+        strips = []
+        for strip in range(2):
+            first = WIDE // TALL * strip + HD // TALL * head
+            strips.append(jnp.concatenate([state[first + k].astype(jnp.float32) for k in range(HD // TALL)], 0))
+        return jnp.concatenate(strips, 1).astype(jnp.bfloat16)
+
     wide = queries[...].astype(jnp.float32).T
     flat[...] = wide
     plain[...] = wide.astype(jnp.bfloat16)
-    both = []
+    tokens = queries.shape[0]
+    products = []
     for head in range(HEADS):
-        product = jnp.zeros((HD, queries.shape[0]), jnp.float32)
+        mine = rows_of(head)
+        product = jnp.zeros((HD, tokens), jnp.float32)
         begin = 0
         for s in range(TURNS + 1):
             value = query_band(flat, plain, head, s)
             end = 2 * s * BAND + value.shape[0]
             feats[head, pl.ds(2 * s * BAND, value.shape[0]), :] = value
             if s != TURNS - 1:
-                here = whole[pl.ds(head * HD, HD), :][:, begin:end].astype(jnp.bfloat16)
                 right = feats[head, pl.ds(begin, end - begin), :]
-                product += jnp.dot(here, right, preferred_element_type=jnp.float32)
+                product += jnp.dot(mine[:, begin:end], right, preferred_element_type=jnp.float32)
                 begin = end
-        both.append(product)
-    result = jnp.concatenate(both, 0) * scale[0]
+        products.append(product)
+    result = jnp.concatenate(products, 0) * scale[0]
     out[...] = result.T.astype(out.dtype)
+    store = pltpu.make_async_copy(out, out_far, sent)
+    store.start()
+    store.wait()
 
 
 def in_vmem():
@@ -155,9 +168,9 @@
             pltpu.VMEM((tokens, WIDE), jnp.bfloat16),
             pltpu.VMEM((PARTS, *part), jnp.bfloat16),
             pltpu.SemaphoreType.DMA((2,)),
-            pltpu.SemaphoreType.DMA((3,)),
+            pltpu.SemaphoreType.DMA((4,)),
         ],
-        compiler_params=pltpu.CompilerParams(vmem_limit_bytes=62 * 2**20),
+        compiler_params=pltpu.CompilerParams(vmem_limit_bytes=60 * 2**20),
         name="state",
     )(keys, values)
 
@@ -168,12 +181,13 @@
         read_kernel,
         out_shape=jax.ShapeDtypeStruct((tokens, WIDE), jnp.bfloat16),
         in_specs=[pl.BlockSpec(memory_space=pltpu.SMEM), in_vmem(), in_vmem()],
-        out_specs=in_vmem(),
+        out_specs=in_hbm(),
         scratch_shapes=[
+            pltpu.VMEM((tokens, WIDE), jnp.bfloat16),
             pltpu.VMEM((WIDE, tokens), jnp.float32),
             pltpu.VMEM((WIDE, tokens), jnp.bfloat16),
             pltpu.VMEM((HEADS, ROWS, tokens), jnp.bfloat16),
-            pltpu.VMEM((WIDE, 2 * STRIP * BAND), jnp.float32),
+            pltpu.SemaphoreType.DMA,
         ],
         compiler_params=pltpu.CompilerParams(vmem_limit_bytes=48 * 2**20),
         name="read",

time: 63.5 us -> 63.3 us (level)
  no operation moved by 1% of the time
where the time goes in v10:
time: 63.3 us; the launch traced here: 63.1 us
  blocking collectives  52.9 us (84%)
  Pallas kernels  9.61 us (15%)
    all_to_all x1, blocking collectives, on_device(): arrived = lax.all_to_all(local, PLANE, 0, 0, tiled=True)  20.6 us
    all_to_all x1, blocking collectives, on_device(): state = lax.all_to_all(copies, PLANE, 0, 0, tiled=True)  17.5 us
    all_to_all x1, blocking collectives, on_device(): others = lax.all_to_all(copies, DEPTH[::-1], 0, 0, tiled=True)  14.8 us
    pallas_call x1, Pallas kernels, make_state(): pl.pallas_call(state_kernel, out_shape=jax.ShapeDtypeStruct((PARTS, *part...  5.31 us
    pallas_call x1, Pallas kernels, read_state(): pl.pallas_call(read_kernel, out_shape=jax.ShapeDtypeStruct((tokens, WIDE)...  4.31 us

profile of v10, /device:TPU:1, one launch (start us, length us, event | category | flops | bytes accessed | tf_op | source)
XLA Modules:
  0.0 63.1 jit_solution(8144367456239539009)
XLA Ops:
  0.1 5.3 %state.1 = bf16[32,8,1152]{2,1,0:T(8,128)(2,1)} custom-call(bf16[2048,128]{1,0:T(8,128)(2,1)} %keys_far.1, bf16[2048,128]{1,0:T(8,128)(2,1)} %values_far.1), custom_call_target="tpu_custom_call" | custom-call | tf_op jit(solution)/shard_map/state/pallas_call | solution.py:161
  5.4 20.6 %all_to_all.15 = bf16[32,8,1152]{2,1,0:T(8,128)(2,1)S(1)} all-to-all(bf16[32,8,1152]{2,1,0:T(8,128)(2,1)} %state.1), channel_id=1, replica_groups=mesh['depth_0'=2,'depth_1'=2,'depth_2'=2,'pair'=2,'core'=2,'near'=2,'row..., dimensions={0} | all-to-all | bytes 1179648 | tf_op jit(solution)/shard_map/all_to_all | solution.py:212
  26.0 0.1 convert_reduce_fusion
  26.1 0.1 reduce_sum.32
  26.2 14.8 %all_to_all.16 = bf16[8,8,1152]{2,1,0:T(8,128)(2,1)S(1)} all-to-all(bf16[8,8,1152]{2,1,0:T(8,128)(2,1)S(1)} %broadcast_in_dim.4), channel_id=1, replica_groups=mesh['depth_0'=2,'depth_1'=2,'depth_2'=2,'pair'=2,'core'=2,'near'=2,'row..., dimensions={0} | all-to-all | bytes 294912 | tf_op jit(solution)/shard_map/all_to_all | solution.py:217
  41.0 0.1 multiply_reduce_fusion
  41.2 0.0 copy-start
  41.2 17.5 %all_to_all.17.state = bf16[32,8,1152]{2,1,0:T(8,128)(2,1)S(1)} all-to-all(bf16[32,8,1152]{2,1,0:T(8,128)(2,1)S(1)} %bitcast.8), channel_id=1, replica_groups=mesh['depth_0'=2,'depth_1'=2,'depth_2'=2,'pair'=2,'core'=2,'near'=2,'row..., dimensions={0} | all-to-all | bytes 1179648 | tf_op jit(solution)/shard_map/all_to_all | solution.py:226
  58.8 0.0 copy-done
  58.8 4.3 %read.1 = bf16[2048,128]{1,0:T(8,128)(2,1)} custom-call(f32[1]{0:T(128)} %bitcast.scale, bf16[2048,128]{1,0:T(8,128)(2,1)S(1)} %copy-done, bf16[32,8,1152]{2,1,0:T(8,128)(2,1)S(1)} %all_to_all.17.state), custom_call_target="tpu_custom_call" | custom-call | tf_op jit(solution)/shard_map/read/pallas_call | solution.py:180
  (6 shorter events, 0.1 us)
Async XLA Ops:
  41.2 17.6 %copy-start = (bf16[2048,128]{1,0:T(8,128)(2,1)S(1)}, bf16[2048,128]{1,0:T(8,128)(2,1)}, u32[]{:S(2)}) copy-start(bf16[2048,128]{1,0:T(8,128)(2,1)} %queries.1) | copy-start | bytes 1572868

commit v11 on v10

--- a/solution.py
+++ b/solution.py
@@ -13,7 +13,7 @@
 BLOCKS = HD // BLOCK
 TURNS = BLOCK // 2
 BAND = 2 * HD
-ROWS = 2 * TURNS * BAND + HD
+ROWS = 2 * TURNS * BAND
 STRIP = 9
 TALL = 8
 PARTS = 2 * WIDE // TALL
@@ -67,17 +67,10 @@
     first = [x, across(wide, False, -1)], [across(wide, True), across(wide, True, -1)]
     lane = lax.broadcasted_iota(jnp.int32, (1, BAND), 1)
 
-    def half_band():
-        feats = jnp.concatenate([first[swap][0] * across(wide, swap == 1, 2) for swap in range(2)], 1)
-        product = jnp.dot(turned_values, feats, preferred_element_type=jnp.float32)
-        heads = []
-        for head in range(HEADS):
-            mine = product[HD * head : HD * head + HD, BAND * head : BAND * head + BAND]
-            heads.append(jnp.where(lane < HD, mine, 0.0))
-        put(2 * TURNS, heads)
-
+    product = jnp.dot(turned_values, x * across(wide, False, 2), preferred_element_type=jnp.float32)
+    heads = [product[HD * head : HD * head + HD] for head in range(HEADS)]
+    put(2 * TURNS, [jnp.where((lane < HD) == (head == 0), heads[head], 0.0) for head in range(HEADS)])
     put(2 * TURNS + 1, [jnp.zeros((HD, BAND), jnp.float32)] * HEADS)
-    half_band()
     store(1, 2 * TURNS - STRIP, STRIP)
     for s in range(TURNS):
         others = across(wide, False, 0, s) if s else x, across(wide, True, 0, s + TURNS)
@@ -125,20 +118,18 @@
     wide = queries[...].astype(jnp.float32).T
     flat[...] = wide
     plain[...] = wide.astype(jnp.bfloat16)
-    tokens = queries.shape[0]
+    mine = [rows_of(head) for head in range(HEADS)]
+    halves = [query_band(flat, plain, head, TURNS) for head in range(HEADS)]
+    last = jnp.concatenate([rows[:, 2 * TURNS * BAND : 2 * TURNS * BAND + BAND] for rows in mine], 0)
+    ends = jnp.dot(last, jnp.concatenate(halves, 0), preferred_element_type=jnp.float32)
     products = []
     for head in range(HEADS):
-        mine = rows_of(head)
-        product = jnp.zeros((HD, tokens), jnp.float32)
-        begin = 0
-        for s in range(TURNS + 1):
-            value = query_band(flat, plain, head, s)
-            end = 2 * s * BAND + value.shape[0]
-            feats[head, pl.ds(2 * s * BAND, value.shape[0]), :] = value
-            if s != TURNS - 1:
-                right = feats[head, pl.ds(begin, end - begin), :]
-                product += jnp.dot(mine[:, begin:end], right, preferred_element_type=jnp.float32)
-                begin = end
+        product = ends[HD * head : HD * head + HD]
+        for s in range(TURNS):
+            here = pl.ds(2 * s * BAND, 2 * BAND)
+            feats[head, here, :] = query_band(flat, plain, head, s)
+            left = mine[head][:, 2 * s * BAND : 2 * s * BAND + 2 * BAND]
+            product += jnp.dot(left, feats[head, here, :], preferred_element_type=jnp.float32)
         products.append(product)
     result = jnp.concatenate(products, 0) * scale[0]
     out[...] = result.T.astype(out.dtype)

time: 63.3 us -> 63.4 us (level)
  no operation moved by 1% of the time
where the time goes in v11:
time: 63.4 us; the launch traced here: 63.1 us
  blocking collectives  52.9 us (83%)
  Pallas kernels  9.68 us (15%)
    all_to_all x1, blocking collectives, on_device(): arrived = lax.all_to_all(local, PLANE, 0, 0, tiled=True)  20.6 us
    all_to_all x1, blocking collectives, on_device(): state = lax.all_to_all(copies, PLANE, 0, 0, tiled=True)  17.5 us
    all_to_all x1, blocking collectives, on_device(): others = lax.all_to_all(copies, DEPTH[::-1], 0, 0, tiled=True)  14.8 us
    pallas_call x1, Pallas kernels, make_state(): pl.pallas_call(state_kernel, out_shape=jax.ShapeDtypeStruct((PARTS, *part...  5.28 us
    pallas_call x1, Pallas kernels, read_state(): pl.pallas_call(read_kernel, out_shape=jax.ShapeDtypeStruct((tokens, WIDE)...  4.4 us

profile of v11, /device:TPU:1, one launch (start us, length us, event | category | flops | bytes accessed | tf_op | source)
XLA Modules:
  0.0 63.1 jit_solution(9858118636937990330)
XLA Ops:
  0.1 5.3 %state.1 = bf16[32,8,1152]{2,1,0:T(8,128)(2,1)} custom-call(bf16[2048,128]{1,0:T(8,128)(2,1)} %keys_far.1, bf16[2048,128]{1,0:T(8,128)(2,1)} %values_far.1), custom_call_target="tpu_custom_call" | custom-call | tf_op jit(solution)/shard_map/state/pallas_call | solution.py:152
  5.4 20.6 %all_to_all.15 = bf16[32,8,1152]{2,1,0:T(8,128)(2,1)S(1)} all-to-all(bf16[32,8,1152]{2,1,0:T(8,128)(2,1)} %state.1), channel_id=1, replica_groups=mesh['depth_0'=2,'depth_1'=2,'depth_2'=2,'pair'=2,'core'=2,'near'=2,'row..., dimensions={0} | all-to-all | bytes 1179648 | tf_op jit(solution)/shard_map/all_to_all | solution.py:203
  26.0 0.1 convert_reduce_fusion
  26.1 0.1 reduce_sum.32
  26.2 14.8 %all_to_all.16 = bf16[8,8,1152]{2,1,0:T(8,128)(2,1)S(1)} all-to-all(bf16[8,8,1152]{2,1,0:T(8,128)(2,1)S(1)} %broadcast_in_dim.4), channel_id=1, replica_groups=mesh['depth_0'=2,'depth_1'=2,'depth_2'=2,'pair'=2,'core'=2,'near'=2,'row..., dimensions={0} | all-to-all | bytes 294912 | tf_op jit(solution)/shard_map/all_to_all | solution.py:208
  41.0 0.1 multiply_reduce_fusion
  41.2 0.0 copy-start
  41.2 17.5 %all_to_all.17.state = bf16[32,8,1152]{2,1,0:T(8,128)(2,1)S(1)} all-to-all(bf16[32,8,1152]{2,1,0:T(8,128)(2,1)S(1)} %bitcast.8), channel_id=1, replica_groups=mesh['depth_0'=2,'depth_1'=2,'depth_2'=2,'pair'=2,'core'=2,'near'=2,'row..., dimensions={0} | all-to-all | bytes 1179648 | tf_op jit(solution)/shard_map/all_to_all | solution.py:217
  58.7 0.0 copy-done
  58.7 4.4 %read.1 = bf16[2048,128]{1,0:T(8,128)(2,1)} custom-call(f32[1]{0:T(128)} %bitcast.scale, bf16[2048,128]{1,0:T(8,128)(2,1)S(1)} %copy-done, bf16[32,8,1152]{2,1,0:T(8,128)(2,1)S(1)} %all_to_all.17.state), custom_call_target="tpu_custom_call" | custom-call | tf_op jit(solution)/shard_map/read/pallas_call | solution.py:171
  (6 shorter events, 0.1 us)
Async XLA Ops:
  41.2 17.6 %copy-start = (bf16[2048,128]{1,0:T(8,128)(2,1)S(1)}, bf16[2048,128]{1,0:T(8,128)(2,1)}, u32[]{:S(2)}) copy-start(bf16[2048,128]{1,0:T(8,128)(2,1)} %queries.1) | copy-start | bytes 1572868

commit v12 on v11

--- a/solution.py
+++ b/solution.py
@@ -16,6 +16,7 @@
 ROWS = 2 * TURNS * BAND
 STRIP = 9
 TALL = 8
+TILE = 2048
 PARTS = 2 * WIDE // TALL
 
 DEPTH = ("depth_0", "depth_1", "depth_2")
@@ -95,47 +96,52 @@
         copy.wait()
 
 
-def query_band(flat, plain, head, s):
-    rows = pl.ds(head * HD, HD)
-    x = plain[rows, :]
-    blocks = [plain[pl.ds(head * HD + k * BLOCK, BLOCK), :] for k in range(BLOCKS)]
+def query_band(wide, x, s):
+    blocks = [x[k * BLOCK : k * BLOCK + BLOCK] for k in range(BLOCKS)]
     if s == TURNS:
         return x * jnp.concatenate(blocks[2:] + blocks[:2], 0)
     lifted = jnp.concatenate(blocks[-1:] + blocks[:-1], 0)
-    turns = (s, s + TURNS) if head == 0 else (s + TURNS, s)
-    others = [pltpu.roll(flat[rows, :], HD - t, 0).astype(jnp.bfloat16) if t else x for t in turns]
-    return jnp.concatenate([first * other for first in (x, lifted) for other in others], 0)
-
-
-def read_kernel(scale, queries, state, out_far, out, flat, plain, feats, sent):
-    def rows_of(head):
-        strips = []
+    others = [pltpu.roll(wide, HD - t, 0).astype(jnp.bfloat16) if t else x for t in (s, s + TURNS)]
+    return [first * other for first in (x, lifted) for other in others]
+
+
+def read_kernel(scale, queries, state, out_far, out, feats, whole, sent):
+    for head in range(HEADS):
         for strip in range(2):
             first = WIDE // TALL * strip + HD // TALL * head
-            strips.append(jnp.concatenate([state[first + k].astype(jnp.float32) for k in range(HD // TALL)], 0))
-        return jnp.concatenate(strips, 1).astype(jnp.bfloat16)
-
-    wide = queries[...].astype(jnp.float32).T
-    flat[...] = wide
-    plain[...] = wide.astype(jnp.bfloat16)
-    mine = [rows_of(head) for head in range(HEADS)]
-    halves = [query_band(flat, plain, head, TURNS) for head in range(HEADS)]
-    last = jnp.concatenate([rows[:, 2 * TURNS * BAND : 2 * TURNS * BAND + BAND] for rows in mine], 0)
-    ends = jnp.dot(last, jnp.concatenate(halves, 0), preferred_element_type=jnp.float32)
-    products = []
-    for head in range(HEADS):
-        product = ends[HD * head : HD * head + HD]
-        for s in range(TURNS):
-            here = pl.ds(2 * s * BAND, 2 * BAND)
-            feats[head, here, :] = query_band(flat, plain, head, s)
-            left = mine[head][:, 2 * s * BAND : 2 * s * BAND + 2 * BAND]
-            product += jnp.dot(left, feats[head, here, :], preferred_element_type=jnp.float32)
-        products.append(product)
-    result = jnp.concatenate(products, 0) * scale[0]
-    out[...] = result.T.astype(out.dtype)
-    store = pltpu.make_async_copy(out, out_far, sent)
-    store.start()
-    store.wait()
+            rows = jnp.concatenate([state[first + k].astype(jnp.float32) for k in range(HD // TALL)], 0)
+            whole[pl.ds(HD * head, HD), pl.ds(STRIP * BAND * strip, STRIP * BAND)] = rows.astype(jnp.bfloat16)
+
+    def store(step):
+        rows = pl.ds(pl.multiple_of(step * TILE, TILE), TILE)
+        return pltpu.make_async_copy(out.at[rows], out_far.at[rows], sent.at[step])
+
+    @pl.loop(0, out.shape[0] // TILE)
+    def _(step):
+        rows = pl.ds(pl.multiple_of(step * TILE, TILE), TILE)
+        wide = queries[rows, :].astype(jnp.float32).T
+        plain = wide.astype(jnp.bfloat16)
+        heads = [pl.ds(HD * head, HD) for head in range(HEADS)]
+        halves = [query_band(None, plain[HD * head : HD * head + HD], TURNS) for head in range(HEADS)]
+        last = whole[:, pl.ds(2 * TURNS * BAND, BAND)]
+        ends = jnp.dot(last, jnp.concatenate(halves, 0), preferred_element_type=jnp.float32)
+        products = []
+        for head in range(HEADS):
+            here = slice(HD * head, HD * head + HD)
+            for s in range(TURNS):
+                parts = query_band(wide[here], plain[here], s)
+                if head == 1:
+                    parts = [parts[k] for k in (1, 0, 3, 2)]
+                feats[head, pl.ds(2 * s * BAND, 2 * BAND), :] = jnp.concatenate(parts, 0)
+            left = whole[heads[head], pl.ds(0, ROWS)]
+            product = jnp.dot(left, feats[head], preferred_element_type=jnp.float32)
+            products.append(ends[here] + product)
+        result = jnp.concatenate(products, 0) * scale[0]
+        out[rows, :] = result.T.astype(out.dtype)
+        store(step).start()
+
+    for step in range(out.shape[0] // TILE):
+        store(step).wait()
 
 
 def in_vmem():
@@ -175,10 +181,9 @@
         out_specs=in_hbm(),
         scratch_shapes=[
             pltpu.VMEM((tokens, WIDE), jnp.bfloat16),
-            pltpu.VMEM((WIDE, tokens), jnp.float32),
-            pltpu.VMEM((WIDE, tokens), jnp.bfloat16),
-            pltpu.VMEM((HEADS, ROWS, tokens), jnp.bfloat16),
-            pltpu.SemaphoreType.DMA,
+            pltpu.VMEM((HEADS, ROWS, TILE), jnp.bfloat16),
+            pltpu.VMEM((WIDE, 2 * STRIP * BAND), jnp.bfloat16),
+            pltpu.SemaphoreType.DMA((tokens // TILE,)),
         ],
         compiler_params=pltpu.CompilerParams(vmem_limit_bytes=48 * 2**20),
         name="read",

time: 63.4 us -> 63.2 us (level)
  no operation moved by 1% of the time
where the time goes in v12:
time: 63.2 us; the launch traced here: 62.9 us
  blocking collectives  52.9 us (84%)
  Pallas kernels  9.45 us (15%)
    all_to_all x1, blocking collectives, on_device(): arrived = lax.all_to_all(local, PLANE, 0, 0, tiled=True)  20.6 us
    all_to_all x1, blocking collectives, on_device(): state = lax.all_to_all(copies, PLANE, 0, 0, tiled=True)  17.5 us
    all_to_all x1, blocking collectives, on_device(): others = lax.all_to_all(copies, DEPTH[::-1], 0, 0, tiled=True)  14.8 us
    pallas_call x1, Pallas kernels, make_state(): pl.pallas_call(state_kernel, out_shape=jax.ShapeDtypeStruct((PARTS, *part...  5.28 us
    pallas_call x1, Pallas kernels, read_state(): pl.pallas_call(read_kernel, out_shape=jax.ShapeDtypeStruct((tokens, WIDE)...  4.17 us

profile of v12, /device:TPU:1, one launch (start us, length us, event | category | flops | bytes accessed | tf_op | source)
XLA Modules:
  0.0 62.9 jit_solution(12607910267803531362)
XLA Ops:
  0.1 5.3 %state.1 = bf16[32,8,1152]{2,1,0:T(8,128)(2,1)} custom-call(bf16[2048,128]{1,0:T(8,128)(2,1)} %keys_far.1, bf16[2048,128]{1,0:T(8,128)(2,1)} %values_far.1), custom_call_target="tpu_custom_call" | custom-call | tf_op jit(solution)/shard_map/state/pallas_call | solution.py:158
  5.4 20.6 %all_to_all.15 = bf16[32,8,1152]{2,1,0:T(8,128)(2,1)S(1)} all-to-all(bf16[32,8,1152]{2,1,0:T(8,128)(2,1)} %state.1), channel_id=1, replica_groups=mesh['depth_0'=2,'depth_1'=2,'depth_2'=2,'pair'=2,'core'=2,'near'=2,'row..., dimensions={0} | all-to-all | bytes 1179648 | tf_op jit(solution)/shard_map/all_to_all | solution.py:208
  26.0 0.1 convert_reduce_fusion
  26.1 0.1 reduce_sum.32
  26.2 14.8 %all_to_all.16 = bf16[8,8,1152]{2,1,0:T(8,128)(2,1)S(1)} all-to-all(bf16[8,8,1152]{2,1,0:T(8,128)(2,1)S(1)} %broadcast_in_dim.4), channel_id=1, replica_groups=mesh['depth_0'=2,'depth_1'=2,'depth_2'=2,'pair'=2,'core'=2,'near'=2,'row..., dimensions={0} | all-to-all | bytes 294912 | tf_op jit(solution)/shard_map/all_to_all | solution.py:213
  41.0 0.1 multiply_reduce_fusion
  41.2 0.0 copy-start
  41.2 17.5 %all_to_all.17.state = bf16[32,8,1152]{2,1,0:T(8,128)(2,1)S(1)} all-to-all(bf16[32,8,1152]{2,1,0:T(8,128)(2,1)S(1)} %bitcast.8), channel_id=1, replica_groups=mesh['depth_0'=2,'depth_1'=2,'depth_2'=2,'pair'=2,'core'=2,'near'=2,'row..., dimensions={0} | all-to-all | bytes 1179648 | tf_op jit(solution)/shard_map/all_to_all | solution.py:222
  58.7 0.0 copy-done
  58.7 4.2 %read.1 = bf16[2048,128]{1,0:T(8,128)(2,1)} custom-call(f32[1]{0:T(128)} %bitcast.scale, bf16[2048,128]{1,0:T(8,128)(2,1)S(1)} %copy-done, bf16[32,8,1152]{2,1,0:T(8,128)(2,1)S(1)} %all_to_all.17.state), custom_call_target="tpu_custom_call" | custom-call | tf_op jit(solution)/shard_map/read/pallas_call | solution.py:177
  (6 shorter events, 0.1 us)
Async XLA Ops:
  41.2 17.6 %copy-start = (bf16[2048,128]{1,0:T(8,128)(2,1)S(1)}, bf16[2048,128]{1,0:T(8,128)(2,1)}, u32[]{:S(2)}) copy-start(bf16[2048,128]{1,0:T(8,128)(2,1)} %queries.1) | copy-start | bytes 1572868

commit v13 on v12

--- a/solution.py
+++ b/solution.py
@@ -20,6 +20,7 @@
 PARTS = 2 * WIDE // TALL
 
 DEPTH = ("depth_0", "depth_1", "depth_2")
+ORDER = (DEPTH[1], DEPTH[2], DEPTH[0])
 PLANE = ("pair", "core", "near", "row")
 EVERY = DEPTH + PLANE
 
@@ -197,10 +198,8 @@
     layers = lax.axis_size(DEPTH)
     count = (lax.axis_index(DEPTH + ("pair", "core")) + 1).astype(jnp.float32)
     scale = (1.0 / (HD * jnp.sqrt(count * (queries.shape[0] * shards)))).reshape(1)
-    order, place = 0, lax.iota(jnp.int32, layers)
-    for axis in DEPTH:
-        size = lax.axis_size(axis)
-        order, place = order * size + place % size, place // size
+    place = lax.iota(jnp.int32, layers)
+    order = 2 * (place // 4) + 1 * (place // 2 % 2) + 4 * (place % 2)
     earlier = (order < lax.axis_index(DEPTH)).astype(jnp.float32)
     local = make_state(keys, values)
     part = local.shape[1:]
@@ -210,7 +209,7 @@
     whole = jnp.sum(totals, 0).astype(jnp.bfloat16)
     copies = jnp.broadcast_to(whole[None], (layers, *part))
     copies, totals, earlier, scale = lax.optimization_barrier((copies, totals, earlier, scale))
-    others = lax.all_to_all(copies, DEPTH[::-1], 0, 0, tiled=True)
+    others = lax.all_to_all(copies, ORDER, 0, 0, tiled=True)
     before = jnp.sum(others.astype(jnp.float32) * earlier[:, None, None], 0)
     running = []
     for group in range(groups):

time: 63.2 us -> 63.1 us (level)
  no operation moved by 1% of the time
where the time goes in v13:
time: 63.1 us; the launch traced here: 62.8 us
  blocking collectives  52.8 us (84%)
  Pallas kernels  9.45 us (15%)
    all_to_all x1, blocking collectives, on_device(): arrived = lax.all_to_all(local, PLANE, 0, 0, tiled=True)  20.6 us
    all_to_all x1, blocking collectives, on_device(): state = lax.all_to_all(copies, PLANE, 0, 0, tiled=True)  17.4 us
    all_to_all x1, blocking collectives, on_device(): others = lax.all_to_all(copies, ORDER, 0, 0, tiled=True)  14.8 us
    pallas_call x1, Pallas kernels, make_state(): pl.pallas_call(state_kernel, out_shape=jax.ShapeDtypeStruct((PARTS, *part...  5.27 us
    pallas_call x1, Pallas kernels, read_state(): pl.pallas_call(read_kernel, out_shape=jax.ShapeDtypeStruct((tokens, WIDE)...  4.18 us

profile of v13, /device:TPU:1, one launch (start us, length us, event | category | flops | bytes accessed | tf_op | source)
XLA Modules:
  0.0 62.8 jit_solution(11573469632640750864)
XLA Ops:
  0.1 5.3 %state.1 = bf16[32,8,1152]{2,1,0:T(8,128)(2,1)} custom-call(bf16[2048,128]{1,0:T(8,128)(2,1)} %keys_far.1, bf16[2048,128]{1,0:T(8,128)(2,1)} %values_far.1), custom_call_target="tpu_custom_call" | custom-call | tf_op jit(solution)/shard_map/state/pallas_call | solution.py:159
  5.4 20.6 %all_to_all.15 = bf16[32,8,1152]{2,1,0:T(8,128)(2,1)S(1)} all-to-all(bf16[32,8,1152]{2,1,0:T(8,128)(2,1)} %state.1), channel_id=1, replica_groups=mesh['depth_0'=2,'depth_1'=2,'depth_2'=2,'pair'=2,'core'=2,'near'=2,'row..., dimensions={0} | all-to-all | bytes 1179648 | tf_op jit(solution)/shard_map/all_to_all | solution.py:207
  26.0 0.1 convert_reduce_fusion
  26.1 0.1 reduce_sum.32
  26.2 14.8 %all_to_all.16 = bf16[8,8,1152]{2,1,0:T(8,128)(2,1)S(1)} all-to-all(bf16[8,8,1152]{2,1,0:T(8,128)(2,1)S(1)} %broadcast_in_dim.4), channel_id=1, replica_groups=mesh['depth_0'=2,'depth_1'=2,'depth_2'=2,'pair'=2,'core'=2,'near'=2,'row..., dimensions={0} | all-to-all | bytes 294912 | tf_op jit(solution)/shard_map/all_to_all | solution.py:212
  41.0 0.1 multiply_reduce_fusion
  41.2 0.0 copy-start
  41.3 17.4 %all_to_all.17.state = bf16[32,8,1152]{2,1,0:T(8,128)(2,1)S(1)} all-to-all(bf16[32,8,1152]{2,1,0:T(8,128)(2,1)S(1)} %bitcast.8), channel_id=1, replica_groups=mesh['depth_0'=2,'depth_1'=2,'depth_2'=2,'pair'=2,'core'=2,'near'=2,'row..., dimensions={0} | all-to-all | bytes 1179648 | tf_op jit(solution)/shard_map/all_to_all | solution.py:221
  58.6 0.0 copy-done
  58.6 4.2 %read.1 = bf16[2048,128]{1,0:T(8,128)(2,1)} custom-call(f32[1]{0:T(128)} %bitcast.scale, bf16[2048,128]{1,0:T(8,128)(2,1)S(1)} %copy-done, bf16[32,8,1152]{2,1,0:T(8,128)(2,1)S(1)} %all_to_all.17.state), custom_call_target="tpu_custom_call" | custom-call | tf_op jit(solution)/shard_map/read/pallas_call | solution.py:178
  (6 shorter events, 0.1 us)
Async XLA Ops:
  41.2 17.4 %copy-start = (bf16[2048,128]{1,0:T(8,128)(2,1)S(1)}, bf16[2048,128]{1,0:T(8,128)(2,1)}, u32[]{:S(2)}) copy-start(bf16[2048,128]{1,0:T(8,128)(2,1)} %queries.1) | copy-start | bytes 1572868

commit v14 on v13

--- a/solution.py
+++ b/solution.py
@@ -21,8 +21,8 @@
 
 DEPTH = ("depth_0", "depth_1", "depth_2")
 ORDER = (DEPTH[1], DEPTH[2], DEPTH[0])
-PLANE = ("pair", "core", "near", "row")
-EVERY = DEPTH + PLANE
+PLANE = ("pair", "core", "row", "near")
+EVERY = DEPTH + ("pair", "core", "near", "row")
 
 
 def across(wide, swap, move=0, turn=0):

time: 63.1 us -> 63.2 us (level)
  no operation moved by 1% of the time
where the time goes in v14:
time: 63.2 us; the launch traced here: 62.9 us
  blocking collectives  52.9 us (84%)
  Pallas kernels  9.45 us (15%)
    all_to_all x1, blocking collectives, on_device(): arrived = lax.all_to_all(local, PLANE, 0, 0, tiled=True)  20.3 us
    all_to_all x1, blocking collectives, on_device(): state = lax.all_to_all(copies, PLANE, 0, 0, tiled=True)  17.8 us
    all_to_all x1, blocking collectives, on_device(): others = lax.all_to_all(copies, ORDER, 0, 0, tiled=True)  14.8 us
    pallas_call x1, Pallas kernels, make_state(): pl.pallas_call(state_kernel, out_shape=jax.ShapeDtypeStruct((PARTS, *part...  5.27 us
    pallas_call x1, Pallas kernels, read_state(): pl.pallas_call(read_kernel, out_shape=jax.ShapeDtypeStruct((tokens, WIDE)...  4.18 us

profile of v14, /device:TPU:1, one launch (start us, length us, event | category | flops | bytes accessed | tf_op | source)
XLA Modules:
  0.0 62.9 jit_solution(15878092777765751620)
XLA Ops:
  0.1 5.3 %state.1 = bf16[32,8,1152]{2,1,0:T(8,128)(2,1)} custom-call(bf16[2048,128]{1,0:T(8,128)(2,1)} %keys_far.1, bf16[2048,128]{1,0:T(8,128)(2,1)} %values_far.1), custom_call_target="tpu_custom_call" | custom-call | tf_op jit(solution)/shard_map/state/pallas_call | solution.py:159
  5.4 20.3 %all_to_all.15 = bf16[32,8,1152]{2,1,0:T(8,128)(2,1)S(1)} all-to-all(bf16[32,8,1152]{2,1,0:T(8,128)(2,1)} %state.1), channel_id=1, replica_groups=mesh['depth_0'=2,'depth_1'=2,'depth_2'=2,'pair'=2,'core'=2,'near'=2,'row..., dimensions={0} | all-to-all | bytes 1179648 | tf_op jit(solution)/shard_map/all_to_all | solution.py:207
  25.7 0.1 convert_reduce_fusion
  25.8 0.1 reduce_sum.32
  25.9 14.8 %all_to_all.16 = bf16[8,8,1152]{2,1,0:T(8,128)(2,1)S(1)} all-to-all(bf16[8,8,1152]{2,1,0:T(8,128)(2,1)S(1)} %broadcast_in_dim.4), channel_id=1, replica_groups=mesh['depth_0'=2,'depth_1'=2,'depth_2'=2,'pair'=2,'core'=2,'near'=2,'row..., dimensions={0} | all-to-all | bytes 294912 | tf_op jit(solution)/shard_map/all_to_all | solution.py:212
  40.7 0.1 multiply_reduce_fusion
  40.9 0.0 copy-start
  40.9 17.8 %all_to_all.17.state = bf16[32,8,1152]{2,1,0:T(8,128)(2,1)S(1)} all-to-all(bf16[32,8,1152]{2,1,0:T(8,128)(2,1)S(1)} %bitcast.8), channel_id=1, replica_groups=mesh['depth_0'=2,'depth_1'=2,'depth_2'=2,'pair'=2,'core'=2,'near'=2,'row..., dimensions={0} | all-to-all | bytes 1179648 | tf_op jit(solution)/shard_map/all_to_all | solution.py:221
  58.7 0.0 copy-done
  58.7 4.2 %read.1 = bf16[2048,128]{1,0:T(8,128)(2,1)} custom-call(f32[1]{0:T(128)} %bitcast.scale, bf16[2048,128]{1,0:T(8,128)(2,1)S(1)} %copy-done, bf16[32,8,1152]{2,1,0:T(8,128)(2,1)S(1)} %all_to_all.17.state), custom_call_target="tpu_custom_call" | custom-call | tf_op jit(solution)/shard_map/read/pallas_call | solution.py:178
  (6 shorter events, 0.1 us)
Async XLA Ops:
  40.9 17.8 %copy-start = (bf16[2048,128]{1,0:T(8,128)(2,1)S(1)}, bf16[2048,128]{1,0:T(8,128)(2,1)}, u32[]{:S(2)}) copy-start(bf16[2048,128]{1,0:T(8,128)(2,1)} %queries.1) | copy-start | bytes 1572868
